TPU v7x, 128 devices: a whole 4x4x4 slice. The times are simulated.
128 devices in a mesh: dp: 16 (over y, x_lo, core), seq: 8 (over z, x_hi).
Axes of the slice: x: 4 (x_hi: 2, x_lo: 2; x = x_hi * 2 + x_lo), y: 4, z: 4, core: 2. Of those that a mesh axis runs over, the one named last changes fastest.
Arguments:
- events: bfloat16 [16, 1024, 1024], P('dp', 'seq'), may hold values from -6 to 6
- in_weight: bfloat16 [1024, 4096], replicated, may hold values from -0.1875 to 0.1875
- out_weight: bfloat16 [1024, 1024], replicated, may hold values from -0.1875 to 0.1875
- rab_table: float32 [18, 8], replicated, may hold values from -4 to 4
- lengths: int32 [16, 4], P('dp'), may hold values from 1 to 512, 1024 in all within a row
- stamps: int32 [16, 1024], P('dp'), may hold values from 0 to 2096128, as said below
- cotangent: bfloat16 [16, 1024, 1024], P('dp', 'seq'), may hold values from -6 to 6
Outputs:
- layer_out: bfloat16 [16, 1024, 1024], P('dp', 'seq')
- input_grad: bfloat16 [16, 1024, 1024], P('dp', 'seq')
- out_weight_grad: float32 [1024, 1024], P(None, ('dp', 'seq'))
- bias_grad: float32 [18, 8], replicated
Inputs may be any that keep to these rules, and one draw needn't show every extreme that they name: Each row holds 4 lengths that sum to 1024; the largest is exactly 512. `stamps`: each row never falls along the history positions, starts at 0 and ends at exactly 2096128.
All inputs are finite; a program needn't handle non-finite values.
Results may differ from a plain program's by a relative error of at most 0.017.
Values may be sent and summed in bfloat16 or wider, within the bound.
A program may use at most 128 MiB of HBM per device.

v0:
```python
import math

import jax
import jax.numpy as jnp
from jax import lax
from jax.sharding import PartitionSpec as P

NORM_EPS = 1e-05


def shifted(value, axis, steps):
    count = lax.axis_size(axis)
    pairs = [(source, (source + steps) % count) for source in range(count)]
    return lax.ppermute(value, axis, pairs)


def silu_parts(values):
    sigmoid_v = jax.nn.sigmoid(values)
    return (values * sigmoid_v, sigmoid_v * (1.0 + values * (1.0 - sigmoid_v)))


def doc_index(positions, doc_ends):
    return jnp.sum((positions[:, None] >= doc_ends[None, :]).astype(jnp.int32), axis=1)


def shard_positions(anchor, row_count, seq_count):
    local = jnp.arange(row_count, dtype=jnp.int32)
    half_rows = row_count // 2
    return jnp.where(
        local < half_rows,
        anchor * half_rows + local,
        (2 * seq_count - 1 - anchor) * half_rows + local - half_rows,
    )


def bucket_onehot(query_stamps, key_stamps, bucket_count):
    stamp_gap = query_stamps[:, None] - key_stamps[None, :]
    levels = 2 ** jnp.arange(bucket_count - 1, dtype=jnp.int32)
    bucket = jnp.sum((stamp_gap[:, :, None] >= levels).astype(jnp.int32), axis=2)
    return (bucket[:, :, None] == jnp.arange(bucket_count, dtype=jnp.int32)).astype(jnp.float32)


def split_heads(rows, head_count):
    return rows.reshape(rows.shape[0], head_count, -1)


def block_scores(query_rows, key_rows, onehot, rab_table, score_scale):
    head_count = rab_table.shape[1]
    raw = jnp.einsum(
        "qhd,khd->hqk",
        split_heads(query_rows, head_count),
        split_heads(key_rows, head_count),
        preferred_element_type=jnp.float32,
    )
    time_bias = jnp.einsum("qkb,bh->hqk", onehot, rab_table, precision=lax.Precision.HIGHEST)
    return raw * score_scale + time_bias


def forward_block(query_rows, key_rows, value_rows, visible, onehot, rab_table, score_scale):
    head_count = rab_table.shape[1]
    scores = block_scores(query_rows, key_rows, onehot, rab_table, score_scale)
    silu_s = scores * jax.nn.sigmoid(scores)
    probs_b = (silu_s * visible[None]).astype(jnp.bfloat16)
    attended = jnp.einsum(
        "hqk,khd->qhd",
        probs_b,
        split_heads(value_rows, head_count),
        preferred_element_type=jnp.float32,
    )
    return attended.reshape(query_rows.shape[0], -1)


def backward_block(
    query_rows, key_rows, value_rows, grad_attn, visible, onehot, rab_table, score_scale
):
    head_count = rab_table.shape[1]
    scores = block_scores(query_rows, key_rows, onehot, rab_table, score_scale)
    silu_s, slope_s = silu_parts(scores)
    probs_b = (silu_s * visible[None]).astype(jnp.bfloat16)
    query_heads = split_heads(query_rows, head_count)
    key_heads = split_heads(key_rows, head_count)
    grad_heads = split_heads(grad_attn, head_count)
    grad_probs = jnp.einsum(
        "qhd,khd->hqk",
        grad_heads,
        split_heads(value_rows, head_count),
        preferred_element_type=jnp.float32,
    )
    grad_scores = grad_probs * visible[None] * slope_s
    grad_scores_b = grad_scores.astype(jnp.bfloat16)
    grad_query = jnp.einsum(
        "hqk,khd->qhd", grad_scores_b, key_heads, preferred_element_type=jnp.float32
    )
    grad_key = jnp.einsum(
        "hqk,qhd->khd", grad_scores_b, query_heads, preferred_element_type=jnp.float32
    )
    grad_value = jnp.einsum("hqk,qhd->khd", probs_b, grad_heads, preferred_element_type=jnp.float32)
    bias_term = jnp.einsum("qkb,hqk->bh", onehot, grad_scores, precision=lax.Precision.HIGHEST)
    return (
        grad_query.reshape(query_rows.shape[0], -1) * score_scale,
        grad_key.reshape(key_rows.shape[0], -1) * score_scale,
        grad_value.reshape(key_rows.shape[0], -1),
        bias_term,
    )


def body(events, in_weight, out_weight, rab_table, lengths, stamps, cotangent):
    event_rows = events[0]
    grad_rows = cotangent[0]
    row_count, width_all = event_rows.shape
    bucket_count, head_count = rab_table.shape
    score_scale = 1.0 / (width_all // head_count) ** 0.5
    seq_count = lax.axis_size("seq")
    seq_index = lax.axis_index("seq")
    norm_scale = 1.0 / math.sqrt(lax.axis_size("dp") * seq_count * row_count)
    doc_ends = jnp.cumsum(lengths[0])
    stamp_row = stamps[0]
    query_pos = shard_positions(seq_index, row_count, seq_count)
    query_stamps = jnp.take(stamp_row, query_pos)
    query_docs = doc_index(query_pos, doc_ends)
    pre_act = jnp.dot(event_rows, in_weight, preferred_element_type=jnp.float32)
    activated, silu_slope = silu_parts(pre_act)
    activated_b = activated.astype(jnp.bfloat16)
    gate_rows = activated_b[:, :width_all]
    value_rows = activated_b[:, width_all : 2 * width_all]
    query_rows = activated_b[:, 2 * width_all : 3 * width_all]
    key_rows = activated_b[:, 3 * width_all :]

    def block_context(anchor):
        key_pos = shard_positions(anchor, row_count, seq_count)
        key_stamps = jnp.take(stamp_row, key_pos)
        same_doc = query_docs[:, None] == doc_index(key_pos, doc_ends)[None, :]
        visible = (same_doc & (key_pos[None, :] <= query_pos[:, None])).astype(jnp.float32)
        return (visible, key_stamps)

    attention = jnp.zeros((row_count, width_all), jnp.float32)
    key_block, value_block = (key_rows, value_rows)
    for step_index in range(seq_count):
        anchor = (seq_index - step_index) % seq_count
        attend_visible, attend_key_stamps = block_context(anchor)

        def attend_compute_block():
            onehot = bucket_onehot(query_stamps, attend_key_stamps, bucket_count)
            return forward_block(
                query_rows, key_block, value_block, attend_visible, onehot, rab_table, score_scale
            )

        def attend_empty_block():
            return jnp.zeros((row_count, width_all), jnp.float32)

        attention = attention + lax.cond(
            jnp.any(attend_visible > 0), attend_compute_block, attend_empty_block
        )
        if step_index + 1 < seq_count:
            key_block, value_block = shifted((key_block, value_block), "seq", 1)
    centre = jnp.mean(attention, axis=1, keepdims=True)
    centred = attention - centre
    sigma = jnp.sqrt(jnp.mean(centred * centred, axis=1, keepdims=True) + NORM_EPS)
    normed = centred / sigma
    gates_f = gate_rows.astype(jnp.float32)
    mixed = (normed * gates_f).astype(jnp.bfloat16)
    layer_out = jnp.dot(mixed, out_weight, preferred_element_type=jnp.float32).astype(jnp.bfloat16)
    grad_mixed = lax.dot_general(
        grad_rows, out_weight, (((1,), (1,)), ((), ())), preferred_element_type=jnp.float32
    )
    grad_gate = grad_mixed * normed
    grad_normed = grad_mixed * gates_f
    grad_attn = (
        (
            grad_normed
            - jnp.mean(grad_normed, axis=1, keepdims=True)
            - normed * jnp.mean(grad_normed * normed, axis=1, keepdims=True)
        )
        / sigma
    ).astype(jnp.bfloat16)

    def attend_back(anchor, key_block, value_block):
        visible, key_stamps = block_context(anchor)

        def compute_block():
            onehot = bucket_onehot(query_stamps, key_stamps, bucket_count)
            return backward_block(
                query_rows,
                key_block,
                value_block,
                grad_attn,
                visible,
                onehot,
                rab_table,
                score_scale,
            )

        def empty_block():
            zero_rows = jnp.zeros((row_count, width_all), jnp.float32)
            return (
                zero_rows,
                zero_rows,
                zero_rows,
                jnp.zeros((bucket_count, head_count), jnp.float32),
            )

        return lax.cond(jnp.any(visible > 0), compute_block, empty_block)

    grad_query = jnp.zeros((row_count, width_all), jnp.float32)
    bias_grad = jnp.zeros((bucket_count, head_count), jnp.float32)
    key_block, value_block = (key_rows, value_rows)
    grad_key = jnp.zeros((row_count, width_all), jnp.float32)
    grad_value = jnp.zeros((row_count, width_all), jnp.float32)
    for step_index in range(seq_count):
        anchor = (seq_index - step_index) % seq_count
        query_term, key_term, value_term, bias_term = attend_back(anchor, key_block, value_block)
        grad_query = grad_query + query_term
        bias_grad = bias_grad + bias_term
        grad_key = grad_key + key_term
        grad_value = grad_value + value_term
        grad_key, grad_value = shifted((grad_key, grad_value), "seq", 1)
        if step_index + 1 < seq_count:
            key_block, value_block = shifted((key_block, value_block), "seq", 1)
    grad_pre = (
        jnp.concatenate([grad_gate, grad_value, grad_query, grad_key], axis=1) * silu_slope
    ).astype(jnp.bfloat16)
    input_grad = lax.dot_general(
        grad_pre, in_weight, (((1,), (1,)), ((), ())), preferred_element_type=jnp.float32
    ).astype(jnp.bfloat16)
    out_term = (
        lax.dot_general(
            mixed, grad_rows, (((0,), (0,)), ((), ())), preferred_element_type=jnp.float32
        )
        * norm_scale
    )
    out_grad = lax.psum_scatter(out_term, ("dp", "seq"), scatter_dimension=1, tiled=True)
    bias_total = lax.psum(bias_grad * norm_scale, ("dp", "seq"))
    return (layer_out[None], input_grad[None], out_grad, bias_total)


def solution(mesh):
    placed = (
        P("dp", "seq", None),
        P(),
        P(),
        P(),
        P("dp", None),
        P("dp", None),
        P("dp", "seq", None),
    )
    return jax.shard_map(
        body,
        mesh=mesh,
        in_specs=placed,
        out_specs=(P("dp", "seq", None), P("dp", "seq", None), P(None, ("dp", "seq")), P()),
        check_vma=False,
    )
```

profile of v0, /device:TPU:0, one launch (start us, length us, event | category | flops | bytes accessed | tf_op | source)
XLA Modules:
  0.0 983.6 jit_solution(11359411267809630758)
XLA Ops:
  7.2 6.3 multiply_convert_fusion.24
  28.4 4.9 collective-permute-done
  39.8 6.4 collective-permute-done.2
  51.0 6.8 collective-permute-done.4
  59.3 4.9 collective-permute-done.7
  64.2 5.3 collective-permute-done.6
  71.2 5.7 collective-permute-done.9
  76.9 5.3 collective-permute-done.8
  88.8 5.8 collective-permute-done.10
  101.4 6.2 conditional.16
  108.1 7.3 conditional.17
  116.2 8.8 conditional.18
  125.0 6.4 conditional.19
  132.2 8.8 conditional.20
  141.0 6.4 conditional.21
  148.2 8.7 conditional.22
  157.0 6.8 conditional.23
  176.1 23.2 %conditional.24 = (f32[128,1024]{0,1:T(8,128)}, f32[128,1024]{0,1:T(8,128)}, f32[18,8]{0,1:T(8,128)S(1)}, f32[128,1024]{1,0:T(8,128)}) conditional(s32[]{:T(128)} %convert_element_type.259, () %tuple.137, (bf16[128,1024]{1,0:T(8,128)(2,1)S(1)}, bf16[128,1024]{1,0:T(8,128)(2,1)}, f32[128,128]{1,0:T(8,128)}, bf16[128,1024]{1,0:T(8,128)(2,1)S(1)}, ...), branch_computations={%region_46.48_spmd, %region_47.50_spmd} | conditional | flops 228573648 | bytes 21039540 | solution.py:202
  204.4 29.1 %conditional.25 = (f32[18,8]{0,1:T(8,128)S(1)}, f32[128,1024]{1,0:T(8,128)}, f32[128,1024]{1,0:T(8,128)}, f32[128,1024]{1,0:T(8,128)}) conditional(s32[]{:T(128)} %convert_element_type.263, () %tuple.139, (bf16[128,1024]{1,0:T(8,128)(2,1)S(1)}, bf16[128,1024]{1,0:T(8,128)(2,1)}, f32[128,128]{1,0:T(8,128)}, bf16[128,1024]{1,0:T(8,128)(2,1)S(1)}, ...), branch_computations={%region_49.51_spmd, %region_50.53_spmd} | conditional | flops 228573648 | bytes 19990908 | solution.py:202
  242.4 30.4 %conditional.26 = (f32[18,8]{0,1:T(8,128)}, f32[128,1024]{1,0:T(8,128)}, f32[128,1024]{1,0:T(8,128)}, f32[128,1024]{1,0:T(8,128)}) conditional(s32[]{:T(128)} %convert_element_type.266, () %tuple.141, (bf16[128,1024]{1,0:T(8,128)(2,1)S(1)}, bf16[128,1024]{1,0:T(8,128)(2,1)}, f32[128,128]{1,0:T(8,128)}, bf16[128,1024]{1,0:T(8,128)(2,1)S(1)}, ...), branch_computations={%region_52.54_spmd, %region_53.56_spmd} | conditional | flops 228573648 | bytes 18942304 | solution.py:202
  282.1 30.7 %conditional.27 = (f32[18,8]{0,1:T(8,128)}, f32[128,1024]{1,0:T(8,128)}, f32[128,1024]{1,0:T(8,128)}, f32[128,1024]{1,0:T(8,128)}) conditional(s32[]{:T(128)} %convert_element_type.269, () %tuple.143, (bf16[128,1024]{1,0:T(8,128)(2,1)S(1)}, bf16[128,1024]{1,0:T(8,128)(2,1)}, f32[128,128]{1,0:T(8,128)}, bf16[128,1024]{1,0:T(8,128)(2,1)S(1)}, ...), branch_computations={%region_55.57_spmd, %region_56.59_spmd} | conditional | flops 228573648 | bytes 18942304 | solution.py:202
  317.0 5.8 collective-permute-start.25
  322.7 30.8 %conditional.28 = (f32[18,8]{0,1:T(8,128)}, f32[128,1024]{1,0:T(8,128)}, f32[128,1024]{1,0:T(8,128)}, f32[128,1024]{1,0:T(8,128)}) conditional(s32[]{:T(128)} %convert_element_type.272, () %tuple.145, (bf16[128,1024]{1,0:T(8,128)(2,1)S(1)}, bf16[128,1024]{1,0:T(8,128)(2,1)}, f32[128,128]{1,0:T(8,128)}, bf16[128,1024]{1,0:T(8,128)(2,1)S(1)}, ...), branch_computations={%region_58.60_spmd, %region_59.62_spmd} | conditional | flops 228573648 | bytes 18942304 | solution.py:202
  358.7 30.6 %conditional.29 = (f32[18,8]{0,1:T(8,128)}, f32[128,1024]{1,0:T(8,128)}, f32[128,1024]{1,0:T(8,128)}, f32[128,1024]{1,0:T(8,128)}) conditional(s32[]{:T(128)} %convert_element_type.275, () %tuple.147, (bf16[128,1024]{1,0:T(8,128)(2,1)S(1)}, bf16[128,1024]{1,0:T(8,128)(2,1)}, f32[128,128]{1,0:T(8,128)}, bf16[128,1024]{1,0:T(8,128)(2,1)S(1)}, ...), branch_computations={%region_61.63_spmd, %region_62.65_spmd} | conditional | flops 228573648 | bytes 18942304 | solution.py:202
  398.1 30.8 %conditional.30 = (f32[18,8]{0,1:T(8,128)}, f32[128,1024]{1,0:T(8,128)}, f32[128,1024]{1,0:T(8,128)}, f32[128,1024]{1,0:T(8,128)}) conditional(s32[]{:T(128)} %convert_element_type.278, () %tuple.149, (bf16[128,1024]{1,0:T(8,128)(2,1)S(1)}, bf16[128,1024]{1,0:T(8,128)(2,1)}, f32[128,128]{1,0:T(8,128)}, bf16[128,1024]{1,0:T(8,128)(2,1)S(1)}, ...), branch_computations={%region_64.66_spmd, %region_65.68_spmd} | conditional | flops 228573648 | bytes 18942304 | solution.py:202
  433.1 5.1 collective-permute-start.28
  438.2 25.1 %conditional.31 = (f32[18,8]{0,1:T(8,128)S(1)}, f32[128,1024]{1,0:T(8,128)}, f32[128,1024]{1,0:T(8,128)}, f32[128,1024]{1,0:T(8,128)}) conditional(s32[]{:T(128)} %convert_element_type.281, () %tuple.151, (bf16[128,1024]{1,0:T(8,128)(2,1)S(1)}, bf16[128,1024]{1,0:T(8,128)(2,1)}, f32[128,128]{1,0:T(8,128)S(1)}, bf16[128,1024]{1,0:T(8,128)(2,1)S(1)}, ...), branch_computations={%region_67.69_spmd, %region_68.71_spmd} | conditional | flops 228573648 | bytes 21825944 | solution.py:202
  464.6 67.2 %psum.7 = f32[18,8]{0,1:T(8,128)} all-reduce(f32[18,8]{0,1:T(8,128)S(1)} %add_multiply_fusion), channel_id=1, replica_groups=mesh['dp'=16,'seq'=8] {'dp','seq'}, use_global_device_ids=true, to_apply=%region_71.73 | all-reduce | flops 144 | bytes 1152 | tf_op jit(solution)/shard_map/psum | solution.py:232
  544.7 7.7 collective-permute-done.21
  552.5 10.9 %collective-permute-done.29 = f32[128,1024]{1,0:T(8,128)S(1)} collective-permute-done((f32[128,1024]{1,0:T(8,128)S(1)}, f32[128,1024]{1,0:T(8,128)S(1)}, u32[]{:S(2)}, u32[]{:S(2)}) %collective-permute-start.29) | collective-permute-done | bytes 524320 | tf_op jit(solution)/shard_map/ppermute | solution.py:14
  563.4 7.0 fusion.306
  570.4 405.8 %reduce-scatter.2.cloned.1.call-done = f32[1024,8]{0,1:T(8,128)} async-done(((f32[1024,1024]{0,1:T(8,128)}), f32[1024,8]{0,1:T(8,128)}) %reduce-scatter.2.cloned.1.call-update) | async-done | bytes 32784 | tf_op jit(solution)/shard_map/reduce_scatter | solution.py:231
  (448 shorter events, 400.7 us)
Async XLA Ops:
  7.2 164.0 %copy-start = (bf16[1024,1024]{1,0:T(8,128)(2,1)S(1)}, bf16[1024,1024]{1,0:T(8,128)(2,1)}, u32[]{:S(2)}) copy-start(bf16[1024,1024]{1,0:T(8,128)(2,1)} %param.43) | copy-start | bytes 6291460
  7.2 969.0 %reduce-scatter.2.cloned.1.call-start = ((), (), s32[]{:S(2)}) async-start(), calls=%async_computation.1 | async-start | bytes 4227072 | tf_op jit(solution)/shard_map/reduce_scatter | solution.py:231
  14.6 13.8 %collective-permute-start.1 = (bf16[128,1024]{1,0:T(8,128)(2,1)S(1)}, bf16[128,1024]{1,0:T(8,128)(2,1)S(1)}, u32[]{:S(2)}, u32[]{:S(2)}) collective-permute-start(bf16[128,1024]{1,0:T(8,128)(2,1)S(1)} %get-tuple-element.916), channel_id=1, source_target_pairs={{0,1},{1,2},{2,3},{3,4},{4,5},{5,6},{6,7},{7,0},{8,9},{9,10},{10,1... | collective-permute-start | bytes 786440 | tf_op jit(solution)/shard_map/ppermute | solution.py:14
  17.7 15.6 %collective-permute-start = (bf16[128,1024]{1,0:T(8,128)(2,1)S(1)}, bf16[128,1024]{1,0:T(8,128)(2,1)}, u32[]{:S(2)}, u32[]{:S(2)}) collective-permute-start(bf16[128,1024]{1,0:T(8,128)(2,1)S(1)} %get-tuple-element.917), channel_id=1, source_target_pairs={{0,1},{1,2},{2,3},{3,4},{4,5},{5,6},{6,7},{7,0},{8,9},{9,10},{10,1... | collective-permute-start | bytes 786440 | tf_op jit(solution)/shard_map/ppermute | solution.py:14
  28.3 10.5 %collective-permute-start.3 = (bf16[128,1024]{1,0:T(8,128)(2,1)S(1)}, bf16[128,1024]{1,0:T(8,128)(2,1)}, u32[]{:S(2)}, u32[]{:S(2)}) collective-permute-start(bf16[128,1024]{1,0:T(8,128)(2,1)S(1)} %collective-permute-done.1), channel_id=1, source_target_pairs={{0,1},{1,2},{2,3},{3,4},{4,5},{5,6},{6,7},{7,0},{8,9},{9,10},{10,1... | collective-permute-start | bytes 786440 | tf_op jit(solution)/shard_map/ppermute | solution.py:14
  33.3 12.9 %collective-permute-start.2 = (bf16[128,1024]{1,0:T(8,128)(2,1)}, bf16[128,1024]{1,0:T(8,128)(2,1)}, u32[]{:S(2)}, u32[]{:S(2)}) collective-permute-start(bf16[128,1024]{1,0:T(8,128)(2,1)} %collective-permute-done), channel_id=1, source_target_pairs={{0,1},{1,2},{2,3},{3,4},{4,5},{5,6},{6,7},{7,0},{8,9},{9,10},{10,1... | collective-permute-start | bytes 786440 | tf_op jit(solution)/shard_map/ppermute | solution.py:14
  38.8 12.2 %collective-permute-start.5 = (bf16[128,1024]{1,0:T(8,128)(2,1)}, bf16[128,1024]{1,0:T(8,128)(2,1)}, u32[]{:S(2)}, u32[]{:S(2)}) collective-permute-start(bf16[128,1024]{1,0:T(8,128)(2,1)} %collective-permute-done.3), channel_id=1, source_target_pairs={{0,1},{1,2},{2,3},{3,4},{4,5},{5,6},{6,7},{7,0},{8,9},{9,10},{10,1... | collective-permute-start | bytes 786440 | tf_op jit(solution)/shard_map/ppermute | solution.py:14
  46.2 11.6 %collective-permute-start.4 = (bf16[128,1024]{1,0:T(8,128)(2,1)}, bf16[128,1024]{1,0:T(8,128)(2,1)}, u32[]{:S(2)}, u32[]{:S(2)}) collective-permute-start(bf16[128,1024]{1,0:T(8,128)(2,1)} %collective-permute-done.2), channel_id=1, source_target_pairs={{0,1},{1,2},{2,3},{3,4},{4,5},{5,6},{6,7},{7,0},{8,9},{9,10},{10,1... | collective-permute-start | bytes 786440 | tf_op jit(solution)/shard_map/ppermute | solution.py:14
  51.0 13.2 %collective-permute-start.7 = (bf16[128,1024]{1,0:T(8,128)(2,1)}, bf16[128,1024]{1,0:T(8,128)(2,1)}, u32[]{:S(2)}, u32[]{:S(2)}) collective-permute-start(bf16[128,1024]{1,0:T(8,128)(2,1)} %collective-permute-done.5), channel_id=1, source_target_pairs={{0,1},{1,2},{2,3},{3,4},{4,5},{5,6},{6,7},{7,0},{8,9},{9,10},{10,1... | collective-permute-start | bytes 786440 | tf_op jit(solution)/shard_map/ppermute | solution.py:14
  57.8 11.6 %collective-permute-start.6 = (bf16[128,1024]{1,0:T(8,128)(2,1)}, bf16[128,1024]{1,0:T(8,128)(2,1)}, u32[]{:S(2)}, u32[]{:S(2)}) collective-permute-start(bf16[128,1024]{1,0:T(8,128)(2,1)} %collective-permute-done.4), channel_id=1, source_target_pairs={{0,1},{1,2},{2,3},{3,4},{4,5},{5,6},{6,7},{7,0},{8,9},{9,10},{10,1... | collective-permute-start | bytes 786440 | tf_op jit(solution)/shard_map/ppermute | solution.py:14
  64.2 12.7 %collective-permute-start.9 = (bf16[128,1024]{1,0:T(8,128)(2,1)}, bf16[128,1024]{1,0:T(8,128)(2,1)}, u32[]{:S(2)}, u32[]{:S(2)}) collective-permute-start(bf16[128,1024]{1,0:T(8,128)(2,1)} %collective-permute-done.7), channel_id=1, source_target_pairs={{0,1},{1,2},{2,3},{3,4},{4,5},{5,6},{6,7},{7,0},{8,9},{9,10},{10,1... | collective-permute-start | bytes 786440 | tf_op jit(solution)/shard_map/ppermute | solution.py:14
  69.4 12.8 %collective-permute-start.8 = (bf16[128,1024]{1,0:T(8,128)(2,1)}, bf16[128,1024]{1,0:T(8,128)(2,1)}, u32[]{:S(2)}, u32[]{:S(2)}) collective-permute-start(bf16[128,1024]{1,0:T(8,128)(2,1)} %collective-permute-done.6), channel_id=1, source_target_pairs={{0,1},{1,2},{2,3},{3,4},{4,5},{5,6},{6,7},{7,0},{8,9},{9,10},{10,1... | collective-permute-start | bytes 786440 | tf_op jit(solution)/shard_map/ppermute | solution.py:14
  76.9 12.0 %collective-permute-start.11 = (bf16[128,1024]{1,0:T(8,128)(2,1)}, bf16[128,1024]{1,0:T(8,128)(2,1)}, u32[]{:S(2)}, u32[]{:S(2)}) collective-permute-start(bf16[128,1024]{1,0:T(8,128)(2,1)} %collective-permute-done.9), channel_id=1, source_target_pairs={{0,1},{1,2},{2,3},{3,4},{4,5},{5,6},{6,7},{7,0},{8,9},{9,10},{10,1... | collective-permute-start | bytes 786440 | tf_op jit(solution)/shard_map/ppermute | solution.py:14
  82.2 12.4 %collective-permute-start.10 = (bf16[128,1024]{1,0:T(8,128)(2,1)}, bf16[128,1024]{1,0:T(8,128)(2,1)}, u32[]{:S(2)}, u32[]{:S(2)}) collective-permute-start(bf16[128,1024]{1,0:T(8,128)(2,1)} %collective-permute-done.8), channel_id=1, source_target_pairs={{0,1},{1,2},{2,3},{3,4},{4,5},{5,6},{6,7},{7,0},{8,9},{9,10},{10,1... | collective-permute-start | bytes 786440 | tf_op jit(solution)/shard_map/ppermute | solution.py:14
  88.8 68.1 %collective-permute-start.13 = (bf16[128,1024]{1,0:T(8,128)(2,1)}, bf16[128,1024]{1,0:T(8,128)(2,1)}, u32[]{:S(2)}, u32[]{:S(2)}) collective-permute-start(bf16[128,1024]{1,0:T(8,128)(2,1)} %collective-permute-done.11), channel_id=1, source_target_pairs={{0,1},{1,2},{2,3},{3,4},{4,5},{5,6},{6,7},{7,0},{8,9},{9,10},{10,1... | collective-permute-start | bytes 786440 | tf_op jit(solution)/shard_map/ppermute | solution.py:14
  94.7 62.3 %collective-permute-start.12 = (bf16[128,1024]{1,0:T(8,128)(2,1)}, bf16[128,1024]{1,0:T(8,128)(2,1)}, u32[]{:S(2)}, u32[]{:S(2)}) collective-permute-start(bf16[128,1024]{1,0:T(8,128)(2,1)} %collective-permute-done.10), channel_id=1, source_target_pairs={{0,1},{1,2},{2,3},{3,4},{4,5},{5,6},{6,7},{7,0},{8,9},{9,10},{10,1... | collective-permute-start | bytes 786440 | tf_op jit(solution)/shard_map/ppermute | solution.py:14
  201.3 32.2 %collective-permute-start.14 = (f32[128,1024]{1,0:T(8,128)}, f32[128,1024]{1,0:T(8,128)}, u32[]{:S(2)}, u32[]{:S(2)}) collective-permute-start(f32[128,1024]{1,0:T(8,128)} %copy.470), channel_id=1, source_target_pairs={{0,1},{1,2},{2,3},{3,4},{4,5},{5,6},{6,7},{7,0},{8,9},{9,10},{10,1... | collective-permute-start | bytes 1572872 | tf_op jit(solution)/shard_map/ppermute | solution.py:14
  204.3 35.9 %collective-permute-start.22 = (f32[128,1024]{1,0:T(8,128)}, f32[128,1024]{1,0:T(8,128)}, u32[]{:S(2)}, u32[]{:S(2)}) collective-permute-start(f32[128,1024]{1,0:T(8,128)} %copy.507), channel_id=1, source_target_pairs={{0,1},{1,2},{2,3},{3,4},{4,5},{5,6},{6,7},{7,0},{8,9},{9,10},{10,1... | collective-permute-start | bytes 1572872 | tf_op jit(solution)/shard_map/ppermute | solution.py:14
  235.6 37.3 %collective-permute-start.15 = (f32[128,1024]{1,0:T(8,128)}, f32[128,1024]{1,0:T(8,128)}, u32[]{:S(2)}, u32[]{:S(2)}) collective-permute-start(f32[128,1024]{1,0:T(8,128)} %add.699), channel_id=1, source_target_pairs={{0,1},{1,2},{2,3},{3,4},{4,5},{5,6},{6,7},{7,0},{8,9},{9,10},{10,1... | collective-permute-start | bytes 1572872 | tf_op jit(solution)/shard_map/ppermute | solution.py:14
  242.3 37.0 %collective-permute-start.23 = (f32[128,1024]{1,0:T(8,128)}, f32[128,1024]{1,0:T(8,128)}, u32[]{:S(2)}, u32[]{:S(2)}) collective-permute-start(f32[128,1024]{1,0:T(8,128)} %add.713), channel_id=1, source_target_pairs={{0,1},{1,2},{2,3},{3,4},{4,5},{5,6},{6,7},{7,0},{8,9},{9,10},{10,1... | collective-permute-start | bytes 1572872 | tf_op jit(solution)/shard_map/ppermute | solution.py:14
  274.9 37.8 %collective-permute-start.16 = (f32[128,1024]{1,0:T(8,128)}, f32[128,1024]{1,0:T(8,128)}, u32[]{:S(2)}, u32[]{:S(2)}) collective-permute-start(f32[128,1024]{1,0:T(8,128)} %add.700), channel_id=1, source_target_pairs={{0,1},{1,2},{2,3},{3,4},{4,5},{5,6},{6,7},{7,0},{8,9},{9,10},{10,1... | collective-permute-start | bytes 1572872 | tf_op jit(solution)/shard_map/ppermute | solution.py:14
  281.3 33.6 %collective-permute-start.24 = (f32[128,1024]{1,0:T(8,128)}, f32[128,1024]{1,0:T(8,128)}, u32[]{:S(2)}, u32[]{:S(2)}) collective-permute-start(f32[128,1024]{1,0:T(8,128)} %add.714), channel_id=1, source_target_pairs={{0,1},{1,2},{2,3},{3,4},{4,5},{5,6},{6,7},{7,0},{8,9},{9,10},{10,1... | collective-permute-start | bytes 1572872 | tf_op jit(solution)/shard_map/ppermute | solution.py:14
  314.9 38.6 %collective-permute-start.17 = (f32[128,1024]{1,0:T(8,128)}, f32[128,1024]{1,0:T(8,128)}, u32[]{:S(2)}, u32[]{:S(2)}) collective-permute-start(f32[128,1024]{1,0:T(8,128)} %add.701), channel_id=1, source_target_pairs={{0,1},{1,2},{2,3},{3,4},{4,5},{5,6},{6,7},{7,0},{8,9},{9,10},{10,1... | collective-permute-start | bytes 1572872 | tf_op jit(solution)/shard_map/ppermute | solution.py:14
  317.0 39.5 %collective-permute-start.25 = (f32[128,1024]{1,0:T(8,128)}, f32[128,1024]{1,0:T(8,128)}, u32[]{:S(2)}, u32[]{:S(2)}) collective-permute-start(f32[128,1024]{1,0:T(8,128)} %add.715), channel_id=1, source_target_pairs={{0,1},{1,2},{2,3},{3,4},{4,5},{5,6},{6,7},{7,0},{8,9},{9,10},{10,1... | collective-permute-start | bytes 1572872 | tf_op jit(solution)/shard_map/ppermute | solution.py:14
  355.6 33.7 %collective-permute-start.18 = (f32[128,1024]{1,0:T(8,128)}, f32[128,1024]{1,0:T(8,128)}, u32[]{:S(2)}, u32[]{:S(2)}) collective-permute-start(f32[128,1024]{1,0:T(8,128)} %add.702), channel_id=1, source_target_pairs={{0,1},{1,2},{2,3},{3,4},{4,5},{5,6},{6,7},{7,0},{8,9},{9,10},{10,1... | collective-permute-start | bytes 1572872 | tf_op jit(solution)/shard_map/ppermute | solution.py:14
  358.6 32.8 %collective-permute-start.26 = (f32[128,1024]{1,0:T(8,128)}, f32[128,1024]{1,0:T(8,128)}, u32[]{:S(2)}, u32[]{:S(2)}) collective-permute-start(f32[128,1024]{1,0:T(8,128)} %add.716), channel_id=1, source_target_pairs={{0,1},{1,2},{2,3},{3,4},{4,5},{5,6},{6,7},{7,0},{8,9},{9,10},{10,1... | collective-permute-start | bytes 1572872 | tf_op jit(solution)/shard_map/ppermute | solution.py:14
  391.3 37.6 %collective-permute-start.19 = (f32[128,1024]{1,0:T(8,128)}, f32[128,1024]{1,0:T(8,128)}, u32[]{:S(2)}, u32[]{:S(2)}) collective-permute-start(f32[128,1024]{1,0:T(8,128)} %add.703), channel_id=1, source_target_pairs={{0,1},{1,2},{2,3},{3,4},{4,5},{5,6},{6,7},{7,0},{8,9},{9,10},{10,1... | collective-permute-start | bytes 1572872 | tf_op jit(solution)/shard_map/ppermute | solution.py:14
  393.5 37.5 %collective-permute-start.27 = (f32[128,1024]{1,0:T(8,128)}, f32[128,1024]{1,0:T(8,128)}, u32[]{:S(2)}, u32[]{:S(2)}) collective-permute-start(f32[128,1024]{1,0:T(8,128)} %add.717), channel_id=1, source_target_pairs={{0,1},{1,2},{2,3},{3,4},{4,5},{5,6},{6,7},{7,0},{8,9},{9,10},{10,1... | collective-permute-start | bytes 1572872 | tf_op jit(solution)/shard_map/ppermute | solution.py:14
  431.0 100.9 %collective-permute-start.20 = (f32[128,1024]{1,0:T(8,128)}, f32[128,1024]{1,0:T(8,128)}, u32[]{:S(2)}, u32[]{:S(2)}) collective-permute-start(f32[128,1024]{1,0:T(8,128)} %add.704), channel_id=1, source_target_pairs={{0,1},{1,2},{2,3},{3,4},{4,5},{5,6},{6,7},{7,0},{8,9},{9,10},{10,1... | collective-permute-start | bytes 1572872 | tf_op jit(solution)/shard_map/ppermute | solution.py:14
  433.1 101.5 %collective-permute-start.28 = (f32[128,1024]{1,0:T(8,128)}, f32[128,1024]{1,0:T(8,128)}, u32[]{:S(2)}, u32[]{:S(2)}) collective-permute-start(f32[128,1024]{1,0:T(8,128)} %add.718), channel_id=1, source_target_pairs={{0,1},{1,2},{2,3},{3,4},{4,5},{5,6},{6,7},{7,0},{8,9},{9,10},{10,1... | collective-permute-start | bytes 1572872 | tf_op jit(solution)/shard_map/ppermute | solution.py:14
  533.1 19.3 %collective-permute-start.21 = (f32[128,1024]{1,0:T(8,128)S(1)}, f32[128,1024]{1,0:T(8,128)S(1)}, u32[]{:S(2)}, u32[]{:S(2)}) collective-permute-start(f32[128,1024]{1,0:T(8,128)S(1)} %add.705), channel_id=1, source_target_pairs={{0,1},{1,2},{2,3},{3,4},{4,5},{5,6},{6,7},{7,0},{8,9},{9,10},{10,1... | collective-permute-start | bytes 1572872 | tf_op jit(solution)/shard_map/ppermute | solution.py:14
  535.9 27.5 %collective-permute-start.29 = (f32[128,1024]{1,0:T(8,128)S(1)}, f32[128,1024]{1,0:T(8,128)S(1)}, u32[]{:S(2)}, u32[]{:S(2)}) collective-permute-start(f32[128,1024]{1,0:T(8,128)S(1)} %add.719), channel_id=1, source_target_pairs={{0,1},{1,2},{2,3},{3,4},{4,5},{5,6},{6,7},{7,0},{8,9},{9,10},{10,1... | collective-permute-start | bytes 1572872 | tf_op jit(solution)/shard_map/ppermute | solution.py:14
  (55 other events, 756.6 us)
Sparse Core Ops, SparseCore 0:
  171.3 804.8 reduce-scatter.1
where the time goes:
time: 997 us; the launch traced here: 984 us
  waiting for transfers between devices  484 us (49%)
  local copies, waits for them, and re-layouts  175 us (18%)
  matrix products  146 us (15%)
  blocking collectives  67.2 us (7%)
  other arithmetic  48.9 us (5%)
  starting transfers between devices  39.8 us (4%)
  between operations  20.2 us (2%)
    reduce_scatter x1, waiting for transfers between devices, body(): lax.psum_scatter(out_term, ('dp', 'seq'), scatter_dimension=1, tiled=True)  406 us
    ppermute x30, waiting for transfers between devices, shifted(): return lax.ppermute(value, axis, pairs)  78.5 us
    psum x1, blocking collectives, body(): bias_total = lax.psum(bias_grad * norm_scale, ('dp', 'seq'))  67.2 us
    cond x24, local copies, waits for them, and re-layouts, attend_back(): return lax.cond(jnp.any(visible > 0), compute_block, empty_block)  48 us
    ppermute x30, starting transfers between devices, shifted(): return lax.ppermute(value, axis, pairs)  39.8 us
    another operation x32, local copies, waits for them, and re-layouts  35.5 us
  transfers between devices with their start and end apart: 31, of which 15 were waited for; matrix products, arithmetic and copies ran while one was open for 35% of the time, Pallas kernels for 0%

commit v1 on v0

v1 whole, which is shorter than its diff:
```python
import functools
import math

import jax
import jax.numpy as jnp
from jax import lax
from jax.experimental import pallas as pl
from jax.experimental.pallas import tpu as pltpu
from jax.sharding import PartitionSpec as P

NORM_EPS = 1e-05
HIDDEN = -1e30
MESH = pl.DeviceIdType.MESH
F32 = jnp.float32
BF16 = jnp.bfloat16

SEQ = 8
ROWS = 128
HALF = 64
LEN = 1024
WIDTH = 1024
HEAD = 128
BUCKETS = 18
STEP = 256


def dot(left, right):
    return jnp.dot(left, right, preferred_element_type=F32)


def dot_t(left, right):
    return lax.dot_general(left, right, (((1,), (1,)), ((), ())), preferred_element_type=F32)


def sigmoid(values):
    return 0.5 * jnp.tanh(0.5 * values) + 0.5


def aligned(value, multiple):
    return pl.multiple_of(value, multiple)


def kernel(
    events_ref,
    in_weight_ref,
    out_weight_ref,
    rab_ref,
    lengths_ref,
    stamps_ref,
    cot_ref,
    layer_out_ref,
    input_grad_ref,
    out_grad_ref,
    bias_grad_ref,
    w_qkv,
    w_gate,
    w_out,
    slope_qkv,
    slope_gate,
    gate_rows,
    grad_mixed,
    gn_rows,
    send_qkv,
    recv_qkv,
    recv_gn,
    query,
    key,
    value,
    gn_head,
    bias,
    bucket,
    slope,
    probs,
    dscores,
    attn,
    stat_send,
    stat_recv,
    normed_head,
    grad_attn,
    query_t,
    grad_attn_t,
    send_normed,
    recv_normed,
    dqkv_head,
    send_dqkv,
    recv_dqkv,
    mixed,
    gp_gate,
    ig_acc,
    cot_t,
    cot_t_other,
    part_own,
    part_send,
    part_recv,
    piece,
    piece_recv,
    hist,
    hist_recv,
    hist_sum,
    hist_all,
    load_sem,
    qkv_ss,
    qkv_rs,
    gn_ss,
    gn_rs,
    stat_ss,
    stat_rs,
    normed_ss,
    normed_rs,
    dqkv_ss,
    dqkv_rs,
    core_ss,
    core_rs,
    part_ss,
    part_rs,
    piece_ss,
    piece_rs,
    hist_ss,
    hist_rs,
    all_ss,
    all_rs,
):
    dp = lax.axis_index("dp")
    seq = lax.axis_index("seq")
    core = lax.rem(dp, 2)
    x_lo = lax.rem(dp // 2, 2)
    y = dp // 4
    other_core = 1 - core
    score_scale = 1.0 / HEAD**0.5
    norm_scale = 1.0 / math.sqrt(16 * LEN)

    def seq_peer(k):
        return (dp, lax.rem(seq + k + 1, SEQ))

    def seq_head(k):
        return lax.rem(seq + k + 1, SEQ)

    def y_index(k):
        return lax.rem(y + k + 1, 4)

    def y_peer(k):
        return (y_index(k) * 4 + lax.rem(dp, 4), seq)

    own_piece = x_lo * SEQ + seq

    def piece_index(k):
        return lax.rem(own_piece + k + 1, 16)

    def piece_peer(k):
        other = piece_index(k)
        return (y * 4 + (other // SEQ) * 2 + core, lax.rem(other, SEQ))

    def dp_peer(k):
        return (lax.rem(dp + k + 1, 16), seq)

    core_peer = (dp + 1 - 2 * core, seq)

    def remote(src, dst, ss, rs, device):
        return pltpu.make_async_remote_copy(
            src_ref=src,
            dst_ref=dst,
            send_sem=ss,
            recv_sem=rs,
            device_id=device,
            device_id_type=MESH,
        )

    events_copy = pltpu.make_async_copy(events_ref.at[0], mixed.at[1], load_sem.at[27])
    events_copy.start()

    def weight_copy(k, p):
        head = seq_head(k)
        return pltpu.make_async_copy(
            in_weight_ref.at[:, pl.ds(aligned((p + 1) * WIDTH + head * HEAD, HEAD), HEAD)],
            w_qkv.at[k, :, pl.ds(p * HEAD, HEAD)],
            load_sem.at[k * 3 + p],
        )

    for k in range(SEQ):
        for p in range(3):
            weight_copy(k, p).start()
    out_weight_copy = pltpu.make_async_copy(out_weight_ref, w_out, load_sem.at[24])
    out_weight_copy.start()
    gate_copy = pltpu.make_async_copy(
        in_weight_ref.at[:, pl.ds(0, WIDTH)], w_gate, load_sem.at[25]
    )
    gate_copy.start()

    barrier = pltpu.get_barrier_semaphore()

    def greet_piece(k, carry):
        pl.semaphore_signal(barrier, inc=1, device_id=piece_peer(k), device_id_type=MESH)
        return carry

    def greet_dp(k, carry):
        pl.semaphore_signal(barrier, inc=1, device_id=dp_peer(k), device_id_type=MESH)
        return carry

    lax.fori_loop(0, 15, greet_piece, 0)
    lax.fori_loop(0, 15, greet_dp, 0)

    events_copy.wait()
    pl.semaphore_wait(barrier, 30)

    def project(k):
        for p in range(3):
            weight_copy(k, p).wait()
        pre = dot(mixed[1], w_qkv[k])
        sig = sigmoid(pre)
        act = pre * sig
        slope_qkv[k] = sig + act * (1.0 - sig)
        return act.astype(BF16)

    def qkv_copy(k):
        return remote(
            send_qkv.at[k], recv_qkv.at[6 - k], qkv_ss.at[k], qkv_rs.at[6 - k], seq_peer(k)
        )

    def project_send(k, carry):
        send_qkv[k] = project(k)
        qkv_copy(k).start()
        return carry

    lax.fori_loop(0, 7, project_send, 0)
    recv_qkv[7] = project(7)

    out_weight_copy.wait()
    gate_copy.wait()
    for c in range(4):
        cols = pl.ds(c * STEP, STEP)
        pre = dot(mixed[1], w_gate[:, cols])
        sig = sigmoid(pre)
        act = pre * sig
        slope_gate[:, cols] = sig + act * (1.0 - sig)
        gate_b = act.astype(BF16)
        gate_rows[:, cols] = gate_b
        gm = dot_t(cot_ref[0], w_out[cols, :])
        grad_mixed[:, cols] = gm
        gn_rows[:, cols] = (gm * gate_b.astype(F32)).astype(BF16)

    def gn_copy(k):
        cols = pl.ds(aligned(seq_head(k) * HEAD, HEAD), HEAD)
        return remote(
            gn_rows.at[:, cols], recv_gn.at[6 - k], gn_ss.at[k], gn_rs.at[6 - k], seq_peer(k)
        )

    def send_gn(k, carry):
        gn_copy(k).start()
        return carry

    lax.fori_loop(0, 7, send_gn, 0)
    recv_gn[7] = gn_rows[:, pl.ds(aligned(seq * HEAD, HEAD), HEAD)]

    for g in range(8):
        tile = jnp.transpose(cot_ref[0, :, pl.ds(g * HEAD, HEAD)])
        cot_t[g, 0] = tile[:HALF]
        cot_t[g, 1] = tile[HALF:]
    cot_copy = remote(
        cot_t.at[:, other_core], cot_t_other, core_ss.at[0], core_rs.at[0], core_peer
    )
    cot_copy.start()

    lane = lax.broadcasted_iota(jnp.int32, (HEAD, HEAD), 1)
    sub = lax.broadcasted_iota(jnp.int32, (HEAD, HEAD), 0)
    table_bucket = jnp.minimum(32 - lane[:8], BUCKETS - 1)
    table = jnp.zeros((8, HEAD), F32)
    for b in range(BUCKETS):
        table = jnp.where(table_bucket == b, rab_ref[b, seq], table)
    table = jnp.broadcast_to(table[:1], (HEAD, HEAD))
    end_0 = lengths_ref[0, 0]
    end_1 = end_0 + lengths_ref[0, 1]
    end_2 = end_1 + lengths_ref[0, 2]
    for i in range(8):
        row_stamp = stamps_ref[:, pl.ds(i * HEAD, HEAD)].astype(F32)
        column_stamp = jnp.transpose(jnp.broadcast_to(row_stamp, (HEAD, HEAD))).astype(jnp.int32)
        row_pos = sub + i * HEAD
        first = jnp.where(
            row_pos >= end_2,
            end_2,
            jnp.where(row_pos >= end_1, end_1, jnp.where(row_pos >= end_0, end_0, 0)),
        )
        for j in range(2 * (i // 2) + 2):
            where = (pl.ds(i * HEAD, HEAD), pl.ds(j * HEAD, HEAD))
            key_pos = lane + j * HEAD
            leading = lax.clz(column_stamp - stamps_ref[:, pl.ds(j * HEAD, HEAD)])
            visible = (key_pos >= first) & (key_pos <= row_pos)
            bias[where] = jnp.where(
                visible, jnp.take_along_axis(table, leading, axis=1), HIDDEN
            )
            bucket[where] = jnp.minimum(32 - leading, BUCKETS - 1)

    def halves(block):
        return (
            pl.ds(aligned(block * HALF, HALF), HALF),
            pl.ds(aligned(LEN - HALF - block * HALF, HALF), HALF),
        )

    def place_qkv(j):
        low, high = halves(seq_head(j))
        for at, rows in ((low, slice(0, HALF)), (high, slice(HALF, ROWS))):
            for p, target in enumerate((value, query, key)):
                target[at, :] = recv_qkv[j, rows, p * HEAD : (p + 1) * HEAD]

    def take_qkv(j, carry):
        qkv_copy(6 - j).wait_recv()
        place_qkv(j)
        return carry

    place_qkv(7)
    lax.fori_loop(0, 7, take_qkv, 0)

    def place_gn(j):
        low, high = halves(seq_head(j))
        gn_head[low, :] = recv_gn[j, :HALF]
        gn_head[high, :] = recv_gn[j, HALF:]

    def take_gn(j, carry):
        gn_copy(6 - j).wait_recv()
        place_gn(j)
        return carry

    for i in range(4):
        rows = pl.ds(i * STEP, STEP)
        for j in range(i + 1):
            cols = pl.ds(j * STEP, STEP)
            scores = dot_t(query[rows, :], key[cols, :]) * score_scale + bias[rows, cols]
            sig = sigmoid(scores)
            silu = scores * sig
            probs[rows, cols] = silu.astype(BF16)
            slope[rows, cols] = sig + silu * (1.0 - sig)
        seen = (i + 1) * STEP
        attn[rows, :] = dot(probs[rows, :seen], value[:seen, :])

    place_gn(7)
    lax.fori_loop(0, 7, take_gn, 0)

    def column_stats(i):
        rows = pl.ds(i * HEAD, HEAD)
        a = attn[rows, :]
        g = gn_head[rows, :].astype(F32)
        mean = jnp.mean(a, axis=1, keepdims=True)
        off = a - mean
        return (
            mean,
            jnp.sum(off * off, axis=1, keepdims=True),
            jnp.sum(g * off, axis=1, keepdims=True),
            jnp.sum(g, axis=1, keepdims=True),
        )

    for i in range(4):
        packed = jnp.zeros((HEAD, HEAD), F32)
        for n, column in enumerate(column_stats(i) + column_stats(i + 4)):
            packed = jnp.where(lane == n, column, packed)
        stat_send[:, pl.ds(i * HEAD, HEAD)] = jnp.transpose(packed)[:8]

    def stat_copy(k):
        return remote(
            stat_send, stat_recv.at[6 - k], stat_ss.at[k], stat_rs.at[6 - k], seq_peer(k)
        )

    def send_stat(k, carry):
        stat_copy(k).start()
        return carry

    lax.fori_loop(0, 7, send_stat, 0)
    stat_recv[7] = stat_send[...]
    for i in range(8):
        rows = pl.ds(i * HEAD, HEAD)
        query_t[:, rows] = jnp.transpose(query[rows, :])

    def take_stat(j, carry):
        stat_copy(6 - j).wait_recv()
        return carry

    lax.fori_loop(0, 7, take_stat, 0)

    for part in range(2):
        rows4 = [[stat_recv[j, part * 4 + n : part * 4 + n + 1, :] for n in range(4)] for j in range(SEQ)]
        mu = sum(r[0] for r in rows4) * (1.0 / SEQ)
        spread = sum(r[1] + HEAD * (r[0] - mu) * (r[0] - mu) for r in rows4)
        inverse = 1.0 / jnp.sqrt(spread * (1.0 / WIDTH) + NORM_EPS)
        along = sum(r[2] + (r[0] - mu) * r[3] for r in rows4) * inverse * (1.0 / WIDTH)
        level = sum(r[3] for r in rows4) * (1.0 / WIDTH)
        for i in range(4):
            at = slice(i * HEAD, (i + 1) * HEAD)
            tile = jnp.where(
                sub == 0,
                mu[:, at],
                jnp.where(sub == 1, inverse[:, at], jnp.where(sub == 2, along[:, at], level[:, at])),
            )
            tile = jnp.transpose(tile)
            rows = pl.ds((part * 4 + i) * HEAD, HEAD)
            normed = (attn[rows, :] - tile[:, 0:1]) * tile[:, 1:2]
            normed_head[rows, :] = normed.astype(BF16)
            grad_attn[rows, :] = (
                (gn_head[rows, :].astype(F32) - tile[:, 3:4] - normed * tile[:, 2:3]) * tile[:, 1:2]
            ).astype(BF16)

    def normed_copy(k):
        return remote(
            send_normed.at[k],
            recv_normed.at[6 - k],
            normed_ss.at[k],
            normed_rs.at[6 - k],
            seq_peer(k),
        )

    def pick_normed(k, target):
        low, high = halves(seq_head(k))
        target[k, :HALF] = normed_head[low, :]
        target[k, HALF:] = normed_head[high, :]

    def send_norm(k, carry):
        pick_normed(k, send_normed)
        normed_copy(k).start()
        return carry

    lax.fori_loop(0, 7, send_norm, 0)
    pick_normed(7, recv_normed)

    for i in range(8):
        rows = pl.ds(i * HEAD, HEAD)
        grad_attn_t[:, rows] = jnp.transpose(grad_attn[rows, :])
    for i in range(4):
        rows = pl.ds(i * STEP, STEP)
        for j in range(i + 1):
            cols = pl.ds(j * STEP, STEP)
            ds = dot_t(grad_attn[rows, :], value[cols, :]) * slope[rows, cols]
            slope[rows, cols] = ds
            dscores[rows, cols] = ds.astype(BF16)
        seen = (i + 1) * STEP
        dqkv_head[rows, HEAD : 2 * HEAD] = (
            dot(dscores[rows, :seen], key[:seen, :]) * score_scale
        ).astype(BF16)
    for j in range(4):
        cols = pl.ds(j * STEP, STEP)
        rest = slice(j * STEP, LEN)
        grad_value = dot(grad_attn_t[:, rest], probs[rest, cols])
        grad_key = dot(query_t[:, rest], dscores[rest, cols]) * score_scale
        dqkv_head[cols, 0:HEAD] = jnp.transpose(grad_value).astype(BF16)
        dqkv_head[cols, 2 * HEAD : 3 * HEAD] = jnp.transpose(grad_key).astype(BF16)

    def dqkv_copy(k):
        return remote(
            send_dqkv.at[k], recv_dqkv.at[6 - k], dqkv_ss.at[k], dqkv_rs.at[6 - k], seq_peer(k)
        )

    def pick_dqkv(k, target):
        low, high = halves(seq_head(k))
        target[k, :HALF] = dqkv_head[low, :]
        target[k, HALF:] = dqkv_head[high, :]

    def send_grad(k, carry):
        pick_dqkv(k, send_dqkv)
        dqkv_copy(k).start()
        return carry

    lax.fori_loop(0, 7, send_grad, 0)
    pick_dqkv(7, recv_dqkv)

    def rows_of_head(j):
        cols = pl.ds(aligned(seq_head(j) * HEAD, HEAD), HEAD)
        normed = recv_normed[j].astype(F32)
        mixed[0, :, cols] = (normed * gate_rows[:, cols].astype(F32)).astype(BF16)
        gp_gate[:, cols] = (grad_mixed[:, cols] * normed * slope_gate[:, cols]).astype(BF16)

    def take_normed(j, carry):
        normed_copy(6 - j).wait_recv()
        rows_of_head(j)
        return carry

    rows_of_head(7)
    lax.fori_loop(0, 7, take_normed, 0)

    ready = remote(
        mixed.at[0], mixed_other_ref(mixed), core_ss.at[1], core_rs.at[1], core_peer
    )
    ready.start()
    for c in range(4):
        cols = pl.ds(c * STEP, STEP)
        layer_out_ref[0, :, cols] = dot(mixed[0], w_out[:, cols]).astype(BF16)
        ig_acc[:, cols] = dot_t(gp_gate[...], w_gate[cols, :])

    cot_copy.wait_recv()
    ready.wait_recv()
    both = mixed_pair(mixed)

    def part_copy(k):
        return remote(
            part_send.at[k], part_recv.at[2 - k], part_ss.at[k], part_rs.at[2 - k], y_peer(k)
        )

    def part_rows(k):
        group = y_index(k) * 2
        left = jnp.concatenate(
            [
                jnp.concatenate([cot_t[group, core], cot_t[group + 1, core]], axis=0),
                jnp.concatenate([cot_t_other[group], cot_t_other[group + 1]], axis=0),
            ],
            axis=1,
        )
        return left

    for k in range(4):
        left = part_rows(k)
        for c in range(4):
            cols = slice(c * STEP, (c + 1) * STEP)
            product = dot(left, both[:, cols])
            if k < 3:
                part_send[k, :, cols] = product.astype(BF16)
            else:
                part_own[:, cols] = product
        if k < 3:
            part_copy(k).start()

    for i in range(4):

        def add_rows(r, sums):
            rows = pl.ds(aligned(i * STEP + r * 8, 8), 8)
            for j in range(2 * (i + 1)):
                cols = pl.ds(j * HEAD, HEAD)
                ds = slope[rows, cols]
                which = bucket[rows, cols]
                sums = tuple(
                    total + jnp.where(which == b, ds, 0.0) for b, total in enumerate(sums)
                )
            return sums

        zeros = tuple(jnp.zeros((8, HEAD), F32) for _ in range(BUCKETS))
        sums = lax.fori_loop(0, STEP // 8, add_rows, zeros if i == 0 else sums)
    hist[...] = jnp.zeros((24, HEAD), F32)
    for b in range(BUCKETS):
        hist[b : b + 1, :] = jnp.sum(sums[b], axis=0, keepdims=True)

    def hist_copy(k):
        return remote(hist, hist_recv.at[14 - k], hist_ss.at[k], hist_rs.at[14 - k], dp_peer(k))

    def send_hist(k, carry):
        hist_copy(k).start()
        return carry

    lax.fori_loop(0, 15, send_hist, 0)

    for k in range(3):
        part_copy(k).wait_recv()
    for g in range(2):
        for c in range(8):
            rows = slice(g * HALF + c * 8, g * HALF + c * 8 + 8)
            total = part_own[rows, :]
            for k in range(3):
                base = g * HALF + (c // 2) * 16
                pair = part_recv[k, base : base + 16, :].astype(F32)
                total = total + pair[(c % 2) * 8 : (c % 2) * 8 + 8]
            piece[g * 8 + c] = jnp.concatenate(
                [total[:, : WIDTH // 2], total[:, WIDTH // 2 :]], axis=0
            ).astype(BF16)

    def piece_copy(k):
        return remote(
            piece.at[piece_index(k)],
            piece_recv.at[14 - k],
            piece_ss.at[k],
            piece_rs.at[14 - k],
            piece_peer(k),
        )

    def send_piece(k, carry):
        piece_copy(k).start()
        return carry

    lax.fori_loop(0, 15, send_piece, 0)

    def take_hist(k, total):
        hist_copy(14 - k).wait_recv()
        return total + hist_recv[k]

    hist_sum[...] = lax.fori_loop(0, 15, take_hist, hist[...]) * norm_scale

    def all_copy(k):
        return remote(hist_sum, hist_all.at[6 - k], all_ss.at[k], all_rs.at[6 - k], seq_peer(k))

    def send_all(k, carry):
        all_copy(k).start()
        return carry

    lax.fori_loop(0, 7, send_all, 0)

    def add_head(j):
        grad_pre = (recv_dqkv[j].astype(F32) * slope_qkv[j]).astype(BF16)
        for c in range(4):
            cols = pl.ds(c * STEP, STEP)
            ig_acc[:, cols] += dot_t(grad_pre, w_qkv[j, cols, :])

    def take_dqkv(j, carry):
        dqkv_copy(6 - j).wait_recv()
        add_head(j)
        return carry

    add_head(7)
    lax.fori_loop(0, 7, take_dqkv, 0)
    input_grad_ref[0] = ig_acc[...].astype(BF16)

    def take_piece(k, total):
        piece_copy(14 - k).wait_recv()
        return total + piece_recv[k].astype(F32)

    total = lax.fori_loop(0, 15, take_piece, piece[own_piece].astype(F32)) * norm_scale
    out_grad_ref[:, : WIDTH // 2] = total[:8]
    out_grad_ref[:, WIDTH // 2 :] = total[8:]

    def head_column(j, table):
        column = jnp.sum(hist_all[j], axis=1, keepdims=True)
        return jnp.where(lane[:24] == seq_head(j), column, table)

    hist_all[7] = hist_sum[...]

    def take_all(j, table):
        all_copy(6 - j).wait_recv()
        return head_column(j, table)

    table = head_column(7, jnp.zeros((24, HEAD), F32))
    bias_grad_ref[...] = lax.fori_loop(0, 7, take_all, table)

    def sent_seq(k, carry):
        for copy in (qkv_copy, gn_copy, stat_copy, normed_copy, dqkv_copy, all_copy):
            copy(k).wait_send()
        return carry

    def sent_many(k, carry):
        piece_copy(k).wait_send()
        hist_copy(k).wait_send()
        return carry

    lax.fori_loop(0, 7, sent_seq, 0)
    lax.fori_loop(0, 15, sent_many, 0)
    for k in range(3):
        part_copy(k).wait_send()
    cot_copy.wait_send()
    ready.wait_send()


def mixed_other_ref(mixed):
    return mixed.at[2]


def mixed_pair(mixed):
    return jnp.concatenate([mixed[0], mixed[2]], axis=0)


def body(events, in_weight, out_weight, rab_table, lengths, stamps, cotangent):
    dma = pltpu.SemaphoreType.DMA
    vmem = pltpu.VMEM
    scratch = [
        vmem((SEQ, WIDTH, 3 * HEAD), BF16),
        vmem((WIDTH, WIDTH), BF16),
        vmem((WIDTH, WIDTH), BF16),
        vmem((SEQ, ROWS, 3 * HEAD), F32),
        vmem((ROWS, WIDTH), F32),
        vmem((ROWS, WIDTH), BF16),
        vmem((ROWS, WIDTH), F32),
        vmem((ROWS, WIDTH), BF16),
        vmem((SEQ, ROWS, 3 * HEAD), BF16),
        vmem((SEQ, ROWS, 3 * HEAD), BF16),
        vmem((SEQ, ROWS, HEAD), BF16),
        vmem((LEN, HEAD), BF16),
        vmem((LEN, HEAD), BF16),
        vmem((LEN, HEAD), BF16),
        vmem((LEN, HEAD), BF16),
        vmem((LEN, LEN), F32),
        vmem((LEN, LEN), jnp.int32),
        vmem((LEN, LEN), F32),
        vmem((LEN, LEN), BF16),
        vmem((LEN, LEN), BF16),
        vmem((LEN, HEAD), F32),
        vmem((8, LEN // 2), F32),
        vmem((SEQ, 8, LEN // 2), F32),
        vmem((LEN, HEAD), BF16),
        vmem((LEN, HEAD), BF16),
        vmem((HEAD, LEN), BF16),
        vmem((HEAD, LEN), BF16),
        vmem((SEQ, ROWS, HEAD), BF16),
        vmem((SEQ, ROWS, HEAD), BF16),
        vmem((LEN, 3 * HEAD), BF16),
        vmem((SEQ, ROWS, 3 * HEAD), BF16),
        vmem((SEQ, ROWS, 3 * HEAD), BF16),
        vmem((3, ROWS, WIDTH), BF16),
        vmem((ROWS, WIDTH), BF16),
        vmem((ROWS, WIDTH), F32),
        vmem((8, 2, HALF, ROWS), BF16),
        vmem((8, HALF, ROWS), BF16),
        vmem((ROWS, WIDTH), F32),
        vmem((3, ROWS, WIDTH), BF16),
        vmem((3, ROWS, WIDTH), BF16),
        vmem((16, 16, WIDTH // 2), BF16),
        vmem((15, 16, WIDTH // 2), BF16),
        vmem((24, HEAD), F32),
        vmem((15, 24, HEAD), F32),
        vmem((24, HEAD), F32),
        vmem((SEQ, 24, HEAD), F32),
        dma((28,)),
        dma((7,)),
        dma((7,)),
        dma((7,)),
        dma((7,)),
        dma((7,)),
        dma((7,)),
        dma((7,)),
        dma((7,)),
        dma((7,)),
        dma((7,)),
        dma((2,)),
        dma((2,)),
        dma((3,)),
        dma((3,)),
        dma((15,)),
        dma((15,)),
        dma((15,)),
        dma((15,)),
        dma((7,)),
        dma((7,)),
    ]
    hbm = pl.BlockSpec(memory_space=pl.ANY)
    local = pl.BlockSpec(memory_space=pltpu.VMEM)
    scalar = pl.BlockSpec(memory_space=pltpu.SMEM)
    layer_out, input_grad, out_grad, bias_grad = pl.pallas_call(
        kernel,
        out_shape=(
            jax.ShapeDtypeStruct((1, ROWS, WIDTH), BF16),
            jax.ShapeDtypeStruct((1, ROWS, WIDTH), BF16),
            jax.ShapeDtypeStruct((8, WIDTH), F32),
            jax.ShapeDtypeStruct((24, HEAD), F32),
        ),
        in_specs=[hbm, hbm, hbm, scalar, scalar, local, local],
        out_specs=(local,) * 4,
        scratch_shapes=scratch,
        compiler_params=pltpu.CompilerParams(
            collective_id=0, has_side_effects=True, vmem_limit_bytes=60 * 2**20
        ),
    )(events, in_weight, out_weight, rab_table, lengths, stamps, cotangent)
    return (layer_out, input_grad, out_grad.T, bias_grad[:BUCKETS, : rab_table.shape[1]])


def solution(mesh):
    placed = (
        P("dp", "seq", None),
        P(),
        P(),
        P(),
        P("dp", None),
        P("dp", None),
        P("dp", "seq", None),
    )
    return jax.shard_map(
        body,
        mesh=mesh,
        in_specs=placed,
        out_specs=(P("dp", "seq", None), P("dp", "seq", None), P(None, ("dp", "seq")), P()),
        check_vma=False,
    )
```

time: 997 us -> 74.8 us (0.08)
  the two profiles are of different devices: /device:TPU:0 before, /device:TPU:1 now
where the time goes in v1:
time: 74.8 us; the launch traced here: 73.8 us
  Pallas kernels  65.7 us (88%)
  local copies, waits for them, and re-layouts  7.45 us (10%)
    pallas_call x1, Pallas kernels, body(): pl.pallas_call(kernel, out_shape=(jax.ShapeDtypeStruct((1, ROWS, WIDTH),...  65.7 us
    unnamed x5, local copies, waits for them, and re-layouts  7.45 us

profile of v1, /device:TPU:1, one launch (start us, length us, event | category | flops | bytes accessed | tf_op | source)
XLA Modules:
  0.0 73.8 jit_solution(16904894355919180370)
XLA Ops:
  0.6 1.4 %copy.11.rab_ref = f32[18,8]{1,0:T(8,128)} copy(f32[18,8]{0,1:T(8,128)} %param.10) | data formatting | bytes 1152 | tf_op args[3]
  2.0 65.7 %shard_map.102 = (bf16[1,128,1024]{2,1,0:T(8,128)(2,1)}, bf16[1,128,1024]{2,1,0:T(8,128)(2,1)}, f32[8,1024]{1,0:T(8,128)}, f32[24,128]{1,0:T(8,128)}) custom-call(bf16[1,128,1024]{2,1,0:T(8,128)(2,1)} %events_ref.1, bf16[1024,4096]{1,0:T(8,128)(2,1)} %in_weight_ref.1, bf16[1024,1024]{1,0:T(8,128)(2,1)} %out_weight_ref.1, f32[18,8]{1,0:T(8,128)} %copy.11.rab_ref, ...), custom_call_target="tpu_custom_call" | custom-call | tf_op jit(solution)/shard_map/pallas_call | solution.py:725
  67.7 1.4 %copy.12 = f32[18,8]{0,1:T(8,128)} copy(f32[18,8]{1,0:T(8,128)} %bitcast.3) | data formatting | bytes 1152
  69.1 1.7 %copy.16 = bf16[1,128,1024]{2,1,0:T(8,128)(2,1)} copy(bf16[1,128,1024]{2,1,0:T(8,128)(2,1)} %get-tuple-element.20) | data formatting | bytes 524288
  70.8 1.7 %copy.17 = bf16[1,128,1024]{2,1,0:T(8,128)(2,1)} copy(bf16[1,128,1024]{2,1,0:T(8,128)(2,1)} %get-tuple-element.21) | data formatting | bytes 524288
  72.4 1.4 %copy.18 = f32[1024,8]{0,1:T(8,128)} copy(f32[1024,8]{0,1:T(8,128)} %bitcast.2) | data formatting | bytes 65536

commit v2 on v1

--- a/solution.py
+++ b/solution.py
@@ -84,20 +84,28 @@
     dqkv_head,
     send_dqkv,
     recv_dqkv,
+    event_rows,
     mixed,
     gp_gate,
     ig_acc,
-    cot_t,
-    cot_t_other,
-    part_own,
-    part_send,
-    part_recv,
+    cot_all,
+    mixed_all,
+    mixed_t,
     piece,
     piece_recv,
+    final_send,
+    final_recv,
     hist,
     hist_recv,
     hist_sum,
     hist_all,
+    rab,
+    lengths,
+    stamps,
+    layer_out_rows,
+    input_grad_rows,
+    store_sem,
+    small_sem,
     load_sem,
     qkv_ss,
     qkv_rs,
@@ -109,10 +117,14 @@
     normed_rs,
     dqkv_ss,
     dqkv_rs,
+    cot_ss,
+    cot_rs,
     core_ss,
     core_rs,
-    part_ss,
-    part_rs,
+    mixed_ss,
+    mixed_rs,
+    final_ss,
+    final_rs,
     piece_ss,
     piece_rs,
     hist_ss,
@@ -125,21 +137,31 @@
     core = lax.rem(dp, 2)
     x_lo = lax.rem(dp // 2, 2)
     y = dp // 4
-    other_core = 1 - core
     score_scale = 1.0 / HEAD**0.5
     norm_scale = 1.0 / math.sqrt(16 * LEN)
 
+    def seq_head(k):
+        along_z = lax.rem(seq // 2 + k - 3 * (k // 4), 4)
+        return along_z * 2 + lax.rem(seq + k + 1, 2)
+
     def seq_peer(k):
-        return (dp, lax.rem(seq + k + 1, SEQ))
-
-    def seq_head(k):
-        return lax.rem(seq + k + 1, SEQ)
-
-    def y_index(k):
-        return lax.rem(y + k + 1, 4)
+        return (dp, seq_head(k))
+
+    def back(k):
+        upper = k // 4
+        return (1 - upper) * lax.rem(8 - k, 4) + upper * (10 - k)
 
     def y_peer(k):
-        return (y_index(k) * 4 + lax.rem(dp, 4), seq)
+        return (lax.rem(y + k + 1, 4) * 4 + lax.rem(dp, 4), seq)
+
+    own_group = y * 2 + core
+
+    def group_index(k):
+        return lax.rem(own_group + k + 1, 8)
+
+    def group_peer(k):
+        other = group_index(k)
+        return ((other // 2) * 4 + x_lo * 2 + lax.rem(other, 2), seq)
 
     own_piece = x_lo * SEQ + seq
 
@@ -165,8 +187,30 @@
             device_id_type=MESH,
         )
 
-    events_copy = pltpu.make_async_copy(events_ref.at[0], mixed.at[1], load_sem.at[27])
+    events_copy = pltpu.make_async_copy(events_ref.at[0], event_rows, load_sem.at[27])
     events_copy.start()
+
+    small_copies = [
+        pltpu.make_async_copy(source, target, small_sem.at[n])
+        for n, (source, target) in enumerate(
+            ((rab_ref, rab), (lengths_ref, lengths), (stamps_ref, stamps))
+        )
+    ]
+    for copy in small_copies:
+        copy.start()
+
+    barrier = pltpu.get_barrier_semaphore()
+
+    def greet_piece(k, carry):
+        pl.semaphore_signal(barrier, inc=1, device_id=piece_peer(k), device_id_type=MESH)
+        return carry
+
+    def greet_dp(k, carry):
+        pl.semaphore_signal(barrier, inc=1, device_id=dp_peer(k), device_id_type=MESH)
+        return carry
+
+    lax.fori_loop(0, 15, greet_piece, 0)
+    lax.fori_loop(0, 15, greet_dp, 0)
 
     def weight_copy(k, p):
         head = seq_head(k)
@@ -185,27 +229,15 @@
         in_weight_ref.at[:, pl.ds(0, WIDTH)], w_gate, load_sem.at[25]
     )
     gate_copy.start()
-
-    barrier = pltpu.get_barrier_semaphore()
-
-    def greet_piece(k, carry):
-        pl.semaphore_signal(barrier, inc=1, device_id=piece_peer(k), device_id_type=MESH)
-        return carry
-
-    def greet_dp(k, carry):
-        pl.semaphore_signal(barrier, inc=1, device_id=dp_peer(k), device_id_type=MESH)
-        return carry
-
-    lax.fori_loop(0, 15, greet_piece, 0)
-    lax.fori_loop(0, 15, greet_dp, 0)
+    cot_load = pltpu.make_async_copy(cot_ref.at[0], cot_all.at[own_group], load_sem.at[26])
+    cot_load.start()
 
     events_copy.wait()
-    pl.semaphore_wait(barrier, 30)
 
     def project(k):
         for p in range(3):
             weight_copy(k, p).wait()
-        pre = dot(mixed[1], w_qkv[k])
+        pre = dot(event_rows[...], w_qkv[k])
         sig = sigmoid(pre)
         act = pre * sig
         slope_qkv[k] = sig + act * (1.0 - sig)
@@ -213,65 +245,83 @@
 
     def qkv_copy(k):
         return remote(
-            send_qkv.at[k], recv_qkv.at[6 - k], qkv_ss.at[k], qkv_rs.at[6 - k], seq_peer(k)
-        )
+            send_qkv.at[k], recv_qkv.at[back(k)], qkv_ss.at[k], qkv_rs.at[back(k)], seq_peer(k)
+        )
+
+    def project_keep(k, carry):
+        send_qkv[k] = project(k)
+        return carry
 
     def project_send(k, carry):
         send_qkv[k] = project(k)
         qkv_copy(k).start()
         return carry
 
-    lax.fori_loop(0, 7, project_send, 0)
+    def send_kept(k, carry):
+        qkv_copy(k).start()
+        return carry
+
+    lax.fori_loop(0, 1, project_keep, 0)
+    pl.semaphore_wait(barrier, 30)
+    lax.fori_loop(0, 1, send_kept, 0)
+    lax.fori_loop(1, 5, project_send, 0)
+    lax.fori_loop(5, 7, project_keep, 0)
     recv_qkv[7] = project(7)
+    qkv_copy(0).wait_send()
+    qkv_copy(5).start()
 
     out_weight_copy.wait()
     gate_copy.wait()
+    cot_load.wait()
     for c in range(4):
         cols = pl.ds(c * STEP, STEP)
-        pre = dot(mixed[1], w_gate[:, cols])
+        pre = dot(event_rows[...], w_gate[:, cols])
         sig = sigmoid(pre)
         act = pre * sig
         slope_gate[:, cols] = sig + act * (1.0 - sig)
         gate_b = act.astype(BF16)
         gate_rows[:, cols] = gate_b
-        gm = dot_t(cot_ref[0], w_out[cols, :])
+        gm = dot_t(cot_all[own_group], w_out[cols, :])
         grad_mixed[:, cols] = gm
         gn_rows[:, cols] = (gm * gate_b.astype(F32)).astype(BF16)
 
     def gn_copy(k):
         cols = pl.ds(aligned(seq_head(k) * HEAD, HEAD), HEAD)
         return remote(
-            gn_rows.at[:, cols], recv_gn.at[6 - k], gn_ss.at[k], gn_rs.at[6 - k], seq_peer(k)
+            gn_rows.at[:, cols], recv_gn.at[back(k)], gn_ss.at[k], gn_rs.at[back(k)], seq_peer(k)
         )
 
     def send_gn(k, carry):
         gn_copy(k).start()
         return carry
 
-    lax.fori_loop(0, 7, send_gn, 0)
     recv_gn[7] = gn_rows[:, pl.ds(aligned(seq * HEAD, HEAD), HEAD)]
-
-    for g in range(8):
-        tile = jnp.transpose(cot_ref[0, :, pl.ds(g * HEAD, HEAD)])
-        cot_t[g, 0] = tile[:HALF]
-        cot_t[g, 1] = tile[HALF:]
-    cot_copy = remote(
-        cot_t.at[:, other_core], cot_t_other, core_ss.at[0], core_rs.at[0], core_peer
-    )
-    cot_copy.start()
+    qkv_copy(1).wait_send()
+    qkv_copy(6).start()
+
+    def cot_copy(k):
+        return remote(
+            cot_all.at[own_group], cot_all.at[own_group], cot_ss.at[k], cot_rs.at[2 - k], y_peer(k)
+        )
+
+    def send_cot(k, carry):
+        cot_copy(k).start()
+        return carry
 
     lane = lax.broadcasted_iota(jnp.int32, (HEAD, HEAD), 1)
     sub = lax.broadcasted_iota(jnp.int32, (HEAD, HEAD), 0)
+    for copy in small_copies:
+        copy.wait()
     table_bucket = jnp.minimum(32 - lane[:8], BUCKETS - 1)
     table = jnp.zeros((8, HEAD), F32)
     for b in range(BUCKETS):
-        table = jnp.where(table_bucket == b, rab_ref[b, seq], table)
+        table = jnp.where(table_bucket == b, rab[seq, b], table)
     table = jnp.broadcast_to(table[:1], (HEAD, HEAD))
-    end_0 = lengths_ref[0, 0]
-    end_1 = end_0 + lengths_ref[0, 1]
-    end_2 = end_1 + lengths_ref[0, 2]
+    end_0 = lengths[0, 0]
+    end_1 = end_0 + lengths[0, 1]
+    end_2 = end_1 + lengths[0, 2]
     for i in range(8):
-        row_stamp = stamps_ref[:, pl.ds(i * HEAD, HEAD)].astype(F32)
+        row_stamp = stamps[:, pl.ds(i * HEAD, HEAD)].astype(F32)
         column_stamp = jnp.transpose(jnp.broadcast_to(row_stamp, (HEAD, HEAD))).astype(jnp.int32)
         row_pos = sub + i * HEAD
         first = jnp.where(
@@ -282,7 +332,7 @@
         for j in range(2 * (i // 2) + 2):
             where = (pl.ds(i * HEAD, HEAD), pl.ds(j * HEAD, HEAD))
             key_pos = lane + j * HEAD
-            leading = lax.clz(column_stamp - stamps_ref[:, pl.ds(j * HEAD, HEAD)])
+            leading = lax.clz(column_stamp - stamps[:, pl.ds(j * HEAD, HEAD)])
             visible = (key_pos >= first) & (key_pos <= row_pos)
             bias[where] = jnp.where(
                 visible, jnp.take_along_axis(table, leading, axis=1), HIDDEN
@@ -302,11 +352,15 @@
                 target[at, :] = recv_qkv[j, rows, p * HEAD : (p + 1) * HEAD]
 
     def take_qkv(j, carry):
-        qkv_copy(6 - j).wait_recv()
+        qkv_copy(back(j)).wait_recv()
         place_qkv(j)
         return carry
 
     place_qkv(7)
+    qkv_copy(2).wait_send()
+    qkv_copy(3).wait_send()
+    lax.fori_loop(0, 7, send_gn, 0)
+    lax.fori_loop(0, 3, send_cot, 0)
     lax.fori_loop(0, 7, take_qkv, 0)
 
     def place_gn(j):
@@ -315,7 +369,7 @@
         gn_head[high, :] = recv_gn[j, HALF:]
 
     def take_gn(j, carry):
-        gn_copy(6 - j).wait_recv()
+        gn_copy(back(j)).wait_recv()
         place_gn(j)
         return carry
 
@@ -355,7 +409,7 @@
 
     def stat_copy(k):
         return remote(
-            stat_send, stat_recv.at[6 - k], stat_ss.at[k], stat_rs.at[6 - k], seq_peer(k)
+            stat_send, stat_recv.at[back(k)], stat_ss.at[k], stat_rs.at[back(k)], seq_peer(k)
         )
 
     def send_stat(k, carry):
@@ -369,7 +423,7 @@
         query_t[:, rows] = jnp.transpose(query[rows, :])
 
     def take_stat(j, carry):
-        stat_copy(6 - j).wait_recv()
+        stat_copy(back(j)).wait_recv()
         return carry
 
     lax.fori_loop(0, 7, take_stat, 0)
@@ -399,9 +453,9 @@
     def normed_copy(k):
         return remote(
             send_normed.at[k],
-            recv_normed.at[6 - k],
+            recv_normed.at[back(k)],
             normed_ss.at[k],
-            normed_rs.at[6 - k],
+            normed_rs.at[back(k)],
             seq_peer(k),
         )
 
@@ -442,7 +496,7 @@
 
     def dqkv_copy(k):
         return remote(
-            send_dqkv.at[k], recv_dqkv.at[6 - k], dqkv_ss.at[k], dqkv_rs.at[6 - k], seq_peer(k)
+            send_dqkv.at[k], recv_dqkv.at[back(k)], dqkv_ss.at[k], dqkv_rs.at[back(k)], seq_peer(k)
         )
 
     def pick_dqkv(k, target):
@@ -455,66 +509,18 @@
         dqkv_copy(k).start()
         return carry
 
-    lax.fori_loop(0, 7, send_grad, 0)
+    lax.fori_loop(0, 5, send_grad, 0)
+    pick_dqkv(5, send_dqkv)
+    pick_dqkv(6, send_dqkv)
     pick_dqkv(7, recv_dqkv)
 
-    def rows_of_head(j):
-        cols = pl.ds(aligned(seq_head(j) * HEAD, HEAD), HEAD)
-        normed = recv_normed[j].astype(F32)
-        mixed[0, :, cols] = (normed * gate_rows[:, cols].astype(F32)).astype(BF16)
-        gp_gate[:, cols] = (grad_mixed[:, cols] * normed * slope_gate[:, cols]).astype(BF16)
-
-    def take_normed(j, carry):
-        normed_copy(6 - j).wait_recv()
-        rows_of_head(j)
-        return carry
-
-    rows_of_head(7)
-    lax.fori_loop(0, 7, take_normed, 0)
-
-    ready = remote(
-        mixed.at[0], mixed_other_ref(mixed), core_ss.at[1], core_rs.at[1], core_peer
-    )
-    ready.start()
-    for c in range(4):
-        cols = pl.ds(c * STEP, STEP)
-        layer_out_ref[0, :, cols] = dot(mixed[0], w_out[:, cols]).astype(BF16)
-        ig_acc[:, cols] = dot_t(gp_gate[...], w_gate[cols, :])
-
-    cot_copy.wait_recv()
-    ready.wait_recv()
-    both = mixed_pair(mixed)
-
-    def part_copy(k):
-        return remote(
-            part_send.at[k], part_recv.at[2 - k], part_ss.at[k], part_rs.at[2 - k], y_peer(k)
-        )
-
-    def part_rows(k):
-        group = y_index(k) * 2
-        left = jnp.concatenate(
-            [
-                jnp.concatenate([cot_t[group, core], cot_t[group + 1, core]], axis=0),
-                jnp.concatenate([cot_t_other[group], cot_t_other[group + 1]], axis=0),
-            ],
-            axis=1,
-        )
-        return left
-
-    for k in range(4):
-        left = part_rows(k)
-        for c in range(4):
-            cols = slice(c * STEP, (c + 1) * STEP)
-            product = dot(left, both[:, cols])
-            if k < 3:
-                part_send[k, :, cols] = product.astype(BF16)
-            else:
-                part_own[:, cols] = product
-        if k < 3:
-            part_copy(k).start()
-
-    for i in range(4):
-
+    for k in range(3):
+        cot_copy(k).wait_recv()
+    pairs = cot_all.reshape(4, 2, ROWS, WIDTH)
+    cot_core = remote(pairs.at[:, core], pairs.at[:, core], core_ss, core_rs, core_peer)
+    cot_core.start()
+
+    def bucket_sums(i, sums):
         def add_rows(r, sums):
             rows = pl.ds(aligned(i * STEP + r * 8, 8), 8)
             for j in range(2 * (i + 1)):
@@ -526,8 +532,56 @@
                 )
             return sums
 
-        zeros = tuple(jnp.zeros((8, HEAD), F32) for _ in range(BUCKETS))
-        sums = lax.fori_loop(0, STEP // 8, add_rows, zeros if i == 0 else sums)
+        return lax.fori_loop(0, STEP // 8, add_rows, sums)
+
+    sums = tuple(jnp.zeros((8, HEAD), F32) for _ in range(BUCKETS))
+    for i in (0, 3):
+        sums = bucket_sums(i, sums)
+    dqkv_copy(0).wait_send()
+    dqkv_copy(5).start()
+    def rows_of_head(j):
+        cols = pl.ds(aligned(seq_head(j) * HEAD, HEAD), HEAD)
+        normed = recv_normed[j].astype(F32)
+        mixed[:, cols] = (normed * gate_rows[:, cols].astype(F32)).astype(BF16)
+        gp_gate[:, cols] = (grad_mixed[:, cols] * normed * slope_gate[:, cols]).astype(BF16)
+
+    def take_normed(j, carry):
+        normed_copy(back(j)).wait_recv()
+        rows_of_head(j)
+        return carry
+
+    rows_of_head(7)
+    lax.fori_loop(0, 7, take_normed, 0)
+
+    def mixed_block(k):
+        return pl.ds(aligned(group_index(k) * HEAD, HEAD), HEAD)
+
+    def mixed_copy(k):
+        return remote(
+            mixed.at[:, mixed_block(k)],
+            mixed_all.at[own_group],
+            mixed_ss.at[k],
+            mixed_rs.at[6 - k],
+            group_peer(k),
+        )
+
+    def send_mixed(k, carry):
+        mixed_copy(k).start()
+        return carry
+
+    lax.fori_loop(0, 7, send_mixed, 0)
+    mixed_all[own_group] = mixed[:, mixed_block(7)]
+    dqkv_copy(1).wait_send()
+    dqkv_copy(6).start()
+    for c in range(4):
+        cols = pl.ds(c * STEP, STEP)
+        layer_out_rows[:, cols] = dot(mixed[...], w_out[:, cols]).astype(BF16)
+        ig_acc[:, cols] = dot_t(gp_gate[...], w_gate[cols, :])
+    layer_out_copy = pltpu.make_async_copy(layer_out_rows, layer_out_ref.at[0], store_sem.at[0])
+    layer_out_copy.start()
+
+    for i in (1, 2):
+        sums = bucket_sums(i, sums)
     hist[...] = jnp.zeros((24, HEAD), F32)
     for b in range(BUCKETS):
         hist[b : b + 1, :] = jnp.sum(sums[b], axis=0, keepdims=True)
@@ -541,19 +595,22 @@
 
     lax.fori_loop(0, 15, send_hist, 0)
 
-    for k in range(3):
-        part_copy(k).wait_recv()
-    for g in range(2):
-        for c in range(8):
-            rows = slice(g * HALF + c * 8, g * HALF + c * 8 + 8)
-            total = part_own[rows, :]
-            for k in range(3):
-                base = g * HALF + (c // 2) * 16
-                pair = part_recv[k, base : base + 16, :].astype(F32)
-                total = total + pair[(c % 2) * 8 : (c % 2) * 8 + 8]
-            piece[g * 8 + c] = jnp.concatenate(
-                [total[:, : WIDTH // 2], total[:, WIDTH // 2 :]], axis=0
-            ).astype(BF16)
+    for k in range(7):
+        mixed_copy(k).wait_recv()
+    cot_core.wait_recv()
+    for g in range(8):
+        mixed_t[:, g * ROWS : (g + 1) * ROWS] = jnp.transpose(mixed_all[g])
+    for c in range(4):
+        cols = slice(c * STEP, (c + 1) * STEP)
+        product = sum(
+            dot(mixed_t[:, q * STEP : (q + 1) * STEP], cot_pair(cot_all, q, cols)) for q in range(4)
+        )
+        for half in range(2):
+            tile = jnp.transpose(product[:, half * HEAD : (half + 1) * HEAD])
+            for t in range(SEQ):
+                piece[half * SEQ + t, c * 16 : (c + 1) * 16, :] = jnp.concatenate(
+                    [tile[t * 8 : t * 8 + 8], tile[HALF + t * 8 : HALF + t * 8 + 8]], axis=0
+                ).astype(BF16)
 
     def piece_copy(k):
         return remote(
@@ -570,21 +627,6 @@
 
     lax.fori_loop(0, 15, send_piece, 0)
 
-    def take_hist(k, total):
-        hist_copy(14 - k).wait_recv()
-        return total + hist_recv[k]
-
-    hist_sum[...] = lax.fori_loop(0, 15, take_hist, hist[...]) * norm_scale
-
-    def all_copy(k):
-        return remote(hist_sum, hist_all.at[6 - k], all_ss.at[k], all_rs.at[6 - k], seq_peer(k))
-
-    def send_all(k, carry):
-        all_copy(k).start()
-        return carry
-
-    lax.fori_loop(0, 7, send_all, 0)
-
     def add_head(j):
         grad_pre = (recv_dqkv[j].astype(F32) * slope_qkv[j]).astype(BF16)
         for c in range(4):
@@ -592,21 +634,55 @@
             ig_acc[:, cols] += dot_t(grad_pre, w_qkv[j, cols, :])
 
     def take_dqkv(j, carry):
-        dqkv_copy(6 - j).wait_recv()
+        dqkv_copy(back(j)).wait_recv()
         add_head(j)
         return carry
 
     add_head(7)
     lax.fori_loop(0, 7, take_dqkv, 0)
-    input_grad_ref[0] = ig_acc[...].astype(BF16)
+    input_grad_rows[...] = ig_acc[...].astype(BF16)
+    input_grad_copy = pltpu.make_async_copy(
+        input_grad_rows, input_grad_ref.at[0], store_sem.at[1]
+    )
+    input_grad_copy.start()
+
+    def take_hist(k, total):
+        hist_copy(14 - k).wait_recv()
+        return total + hist_recv[k]
+
+    hist_sum[...] = lax.fori_loop(0, 15, take_hist, hist[...]) * norm_scale
+
+    def all_copy(k):
+        return remote(hist_sum, hist_all.at[back(k)], all_ss.at[k], all_rs.at[back(k)], seq_peer(k))
+
+    def send_all(k, carry):
+        all_copy(k).start()
+        return carry
+
+    lax.fori_loop(0, 7, send_all, 0)
 
     def take_piece(k, total):
         piece_copy(14 - k).wait_recv()
         return total + piece_recv[k].astype(F32)
 
     total = lax.fori_loop(0, 15, take_piece, piece[own_piece].astype(F32)) * norm_scale
-    out_grad_ref[:, : WIDTH // 2] = total[:8]
-    out_grad_ref[:, WIDTH // 2 :] = total[8:]
+    final_send[...] = total.reshape(8, 8, HEAD)
+
+    def final_copy(k):
+        return remote(
+            final_send.at[group_index(k)],
+            final_recv.at[own_group],
+            final_ss.at[k],
+            final_rs.at[6 - k],
+            group_peer(k),
+        )
+
+    def send_final(k, carry):
+        final_copy(k).start()
+        return carry
+
+    lax.fori_loop(0, 7, send_final, 0)
+    final_recv[own_group] = final_send[own_group]
 
     def head_column(j, table):
         column = jnp.sum(hist_all[j], axis=1, keepdims=True)
@@ -615,14 +691,21 @@
     hist_all[7] = hist_sum[...]
 
     def take_all(j, table):
-        all_copy(6 - j).wait_recv()
+        all_copy(back(j)).wait_recv()
         return head_column(j, table)
 
     table = head_column(7, jnp.zeros((24, HEAD), F32))
-    bias_grad_ref[...] = lax.fori_loop(0, 7, take_all, table)
+    table = lax.fori_loop(0, 7, take_all, table)
+    table = jnp.transpose(jnp.concatenate([table, jnp.zeros((HEAD - 24, HEAD), F32)], axis=0))
+    bias_grad_ref[...] = table[:8, :BUCKETS]
+
+    for k in range(7):
+        final_copy(k).wait_recv()
+    for g in range(8):
+        out_grad_ref[:, g * HEAD : (g + 1) * HEAD] = final_recv[g]
 
     def sent_seq(k, carry):
-        for copy in (qkv_copy, gn_copy, stat_copy, normed_copy, dqkv_copy, all_copy):
+        for copy in (gn_copy, stat_copy, normed_copy, mixed_copy, all_copy, final_copy):
             copy(k).wait_send()
         return carry
 
@@ -634,17 +717,24 @@
     lax.fori_loop(0, 7, sent_seq, 0)
     lax.fori_loop(0, 15, sent_many, 0)
     for k in range(3):
-        part_copy(k).wait_send()
-    cot_copy.wait_send()
-    ready.wait_send()
-
-
-def mixed_other_ref(mixed):
-    return mixed.at[2]
-
-
-def mixed_pair(mixed):
-    return jnp.concatenate([mixed[0], mixed[2]], axis=0)
+        cot_copy(k).wait_send()
+    cot_core.wait_send()
+    for k in range(4, 7):
+        qkv_copy(k).wait_send()
+    for k in range(2, 7):
+        dqkv_copy(k).wait_send()
+    layer_out_copy.wait()
+    input_grad_copy.wait()
+
+
+def cot_pair(cot_all, q, cols):
+    return jnp.concatenate([cot_all[2 * q, :, cols], cot_all[2 * q + 1, :, cols]], axis=0)
+
+
+def finish(*refs):
+    count = len(refs) // 2
+    for source, target in zip(refs[:count], refs[count:]):
+        target[...] = source[...]
 
 
 def body(events, in_weight, out_weight, rab_table, lengths, stamps, cotangent):
@@ -683,35 +773,47 @@
         vmem((LEN, 3 * HEAD), BF16),
         vmem((SEQ, ROWS, 3 * HEAD), BF16),
         vmem((SEQ, ROWS, 3 * HEAD), BF16),
-        vmem((3, ROWS, WIDTH), BF16),
+        vmem((ROWS, WIDTH), BF16),
+        vmem((ROWS, WIDTH), BF16),
         vmem((ROWS, WIDTH), BF16),
         vmem((ROWS, WIDTH), F32),
-        vmem((8, 2, HALF, ROWS), BF16),
-        vmem((8, HALF, ROWS), BF16),
-        vmem((ROWS, WIDTH), F32),
-        vmem((3, ROWS, WIDTH), BF16),
-        vmem((3, ROWS, WIDTH), BF16),
-        vmem((16, 16, WIDTH // 2), BF16),
-        vmem((15, 16, WIDTH // 2), BF16),
+        vmem((8, ROWS, WIDTH), BF16),
+        vmem((8, ROWS, HEAD), BF16),
+        vmem((HEAD, 8 * ROWS), BF16),
+        vmem((16, HALF, HEAD), BF16),
+        vmem((15, HALF, HEAD), BF16),
+        vmem((8, 8, HEAD), F32),
+        vmem((8, 8, HEAD), F32),
         vmem((24, HEAD), F32),
         vmem((15, 24, HEAD), F32),
         vmem((24, HEAD), F32),
         vmem((SEQ, 24, HEAD), F32),
-        dma((28,)),
-        dma((7,)),
-        dma((7,)),
-        dma((7,)),
-        dma((7,)),
-        dma((7,)),
-        dma((7,)),
-        dma((7,)),
-        dma((7,)),
-        dma((7,)),
-        dma((7,)),
-        dma((2,)),
+        pltpu.SMEM((SEQ, BUCKETS), F32),
+        pltpu.SMEM((1, 4), jnp.int32),
+        vmem((1, LEN), jnp.int32),
+        vmem((ROWS, WIDTH), BF16),
+        vmem((ROWS, WIDTH), BF16),
         dma((2,)),
         dma((3,)),
+        dma((28,)),
+        dma((7,)),
+        dma((7,)),
+        dma((7,)),
+        dma((7,)),
+        dma((7,)),
+        dma((7,)),
+        dma((7,)),
+        dma((7,)),
+        dma((7,)),
+        dma((7,)),
         dma((3,)),
+        dma((3,)),
+        dma,
+        dma,
+        dma((7,)),
+        dma((7,)),
+        dma((7,)),
+        dma((7,)),
         dma((15,)),
         dma((15,)),
         dma((15,)),
@@ -721,23 +823,29 @@
     ]
     hbm = pl.BlockSpec(memory_space=pl.ANY)
     local = pl.BlockSpec(memory_space=pltpu.VMEM)
-    scalar = pl.BlockSpec(memory_space=pltpu.SMEM)
-    layer_out, input_grad, out_grad, bias_grad = pl.pallas_call(
+    shapes = (
+        jax.ShapeDtypeStruct((1, ROWS, WIDTH), BF16),
+        jax.ShapeDtypeStruct((1, ROWS, WIDTH), BF16),
+        jax.ShapeDtypeStruct((8, WIDTH), F32),
+        jax.ShapeDtypeStruct((SEQ, BUCKETS), F32),
+    )
+    results = pl.pallas_call(
         kernel,
-        out_shape=(
-            jax.ShapeDtypeStruct((1, ROWS, WIDTH), BF16),
-            jax.ShapeDtypeStruct((1, ROWS, WIDTH), BF16),
-            jax.ShapeDtypeStruct((8, WIDTH), F32),
-            jax.ShapeDtypeStruct((24, HEAD), F32),
-        ),
-        in_specs=[hbm, hbm, hbm, scalar, scalar, local, local],
-        out_specs=(local,) * 4,
+        out_shape=shapes,
+        in_specs=[hbm] * 7,
+        out_specs=(hbm, hbm, local, local),
         scratch_shapes=scratch,
         compiler_params=pltpu.CompilerParams(
             collective_id=0, has_side_effects=True, vmem_limit_bytes=60 * 2**20
         ),
-    )(events, in_weight, out_weight, rab_table, lengths, stamps, cotangent)
-    return (layer_out, input_grad, out_grad.T, bias_grad[:BUCKETS, : rab_table.shape[1]])
+    )(events, in_weight, out_weight, rab_table.T, lengths, stamps, cotangent)
+    layer_out, input_grad, out_grad, bias_grad = pl.pallas_call(
+        finish,
+        out_shape=shapes,
+        in_specs=[local] * 4,
+        out_specs=(local,) * 4,
+    )(*results)
+    return (layer_out, input_grad, out_grad.T, bias_grad.T)
 
 
 def solution(mesh):

time: 74.8 us -> 60 us (0.80); the launches traced: 73.8 us -> 59.9 us
  local copies, waits for them, and re-layouts: 7.45 us -> 0 us
  Pallas kernels: 65.7 us -> 59.2 us
    unnamed x5 -> x0, local copies, waits for them, and re-layouts: 7.45 us -> none
    pallas_call x1 -> x2, Pallas kernels: 65.7 us -> 59.2 us  [the longest x1 57.4 us: body(): pl.pallas_call(kernel, out_shape=shapes, in_specs=[hbm] * 7, out_specs=(h...]
where the time goes in v2:
time: 60 us; the launch traced here: 59.9 us
  Pallas kernels  59.2 us (99%)
  between operations  0.64 us (1%)
    pallas_call x1, Pallas kernels, body(): pl.pallas_call(kernel, out_shape=shapes, in_specs=[hbm] * 7, out_specs=(h...  57.4 us
    pallas_call x1, Pallas kernels, body(): pl.pallas_call(finish, out_shape=shapes, in_specs=[local] * 4, out_specs=...  1.85 us

profile of v2, /device:TPU:1, one launch (start us, length us, event | category | flops | bytes accessed | tf_op | source)
XLA Modules:
  0.0 59.9 jit_solution(7724233782081078159)
XLA Ops:
  0.6 57.4 %shard_map.102 = (bf16[1,128,1024]{2,1,0:T(8,128)(2,1)}, bf16[1,128,1024]{2,1,0:T(8,128)(2,1)}, f32[8,1024]{1,0:T(8,128)}, f32[8,18]{1,0:T(8,128)}) custom-call(bf16[1,128,1024]{2,1,0:T(8,128)(2,1)} %events_ref.1, bf16[1024,4096]{1,0:T(8,128)(2,1)} %in_weight_ref.1, bf16[1024,1024]{1,0:T(8,128)(2,1)} %out_weight_ref.1, f32[8,18]{1,0:T(8,128)} %bitcast.3, ...), custom_call_target="tpu_custom_call" | custom-call | tf_op jit(solution)/shard_map/pallas_call | solution.py:832
  58.0 1.8 %shard_map.103 = (bf16[1,128,1024]{2,1,0:T(8,128)(2,1)}, bf16[1,128,1024]{2,1,0:T(8,128)(2,1)}, f32[8,1024]{1,0:T(8,128)}, f32[8,18]{1,0:T(8,128)}) custom-call(bf16[1,128,1024]{2,1,0:T(8,128)(2,1)} %get-tuple-element.12.refs_0_, bf16[1,128,1024]{2,1,0:T(8,128)(2,1)} %get-tuple-element.13.refs_1_, f32[8,1024]{1,0:T(8,128)} %get-tuple-element.14.refs_2_, ...), custom_call_target="tpu_custom_call" | custom-call | tf_op jit(solution)/shard_map/pallas_call | solution.py:842

commit v3 on v2

--- a/solution.py
+++ b/solution.py
@@ -34,6 +34,10 @@
 
 def sigmoid(values):
     return 0.5 * jnp.tanh(0.5 * values) + 0.5
+
+
+def pick_lane(values, lanes):
+    return jnp.take_along_axis(values, lanes, axis=1, mode="promise_in_bounds")
 
 
 def aligned(value, multiple):
@@ -75,12 +79,13 @@
     attn,
     stat_send,
     stat_recv,
-    normed_head,
+    centred_head,
+    row_stats,
     grad_attn,
     query_t,
     grad_attn_t,
-    send_normed,
-    recv_normed,
+    send_centred,
+    recv_centred,
     dqkv_head,
     send_dqkv,
     recv_dqkv,
@@ -95,9 +100,7 @@
     piece_recv,
     final_send,
     final_recv,
-    hist,
     hist_recv,
-    hist_sum,
     hist_all,
     rab,
     lengths,
@@ -113,8 +116,8 @@
     gn_rs,
     stat_ss,
     stat_rs,
-    normed_ss,
-    normed_rs,
+    centred_ss,
+    centred_rs,
     dqkv_ss,
     dqkv_rs,
     cot_ss,
@@ -172,9 +175,6 @@
         other = piece_index(k)
         return (y * 4 + (other // SEQ) * 2 + core, lax.rem(other, SEQ))
 
-    def dp_peer(k):
-        return (lax.rem(dp + k + 1, 16), seq)
-
     core_peer = (dp + 1 - 2 * core, seq)
 
     def remote(src, dst, ss, rs, device):
@@ -187,7 +187,10 @@
             device_id_type=MESH,
         )
 
-    events_copy = pltpu.make_async_copy(events_ref.at[0], event_rows, load_sem.at[27])
+    def wait_bytes(ref, sem):
+        pltpu.make_async_copy(ref, ref, sem).wait()
+
+    events_copy = pltpu.make_async_copy(events_ref.at[0], event_rows, load_sem.at[11])
     events_copy.start()
 
     small_copies = [
@@ -205,38 +208,37 @@
         pl.semaphore_signal(barrier, inc=1, device_id=piece_peer(k), device_id_type=MESH)
         return carry
 
-    def greet_dp(k, carry):
-        pl.semaphore_signal(barrier, inc=1, device_id=dp_peer(k), device_id_type=MESH)
+    def greet_group(k, carry):
+        pl.semaphore_signal(barrier, inc=1, device_id=group_peer(k), device_id_type=MESH)
         return carry
 
     lax.fori_loop(0, 15, greet_piece, 0)
-    lax.fori_loop(0, 15, greet_dp, 0)
+    lax.fori_loop(0, 7, greet_group, 0)
 
     def weight_copy(k, p):
         head = seq_head(k)
         return pltpu.make_async_copy(
             in_weight_ref.at[:, pl.ds(aligned((p + 1) * WIDTH + head * HEAD, HEAD), HEAD)],
             w_qkv.at[k, :, pl.ds(p * HEAD, HEAD)],
-            load_sem.at[k * 3 + p],
+            load_sem.at[k],
         )
 
     for k in range(SEQ):
         for p in range(3):
             weight_copy(k, p).start()
-    out_weight_copy = pltpu.make_async_copy(out_weight_ref, w_out, load_sem.at[24])
+    out_weight_copy = pltpu.make_async_copy(out_weight_ref, w_out, load_sem.at[8])
     out_weight_copy.start()
     gate_copy = pltpu.make_async_copy(
-        in_weight_ref.at[:, pl.ds(0, WIDTH)], w_gate, load_sem.at[25]
+        in_weight_ref.at[:, pl.ds(0, WIDTH)], w_gate, load_sem.at[9]
     )
     gate_copy.start()
-    cot_load = pltpu.make_async_copy(cot_ref.at[0], cot_all.at[own_group], load_sem.at[26])
+    cot_load = pltpu.make_async_copy(cot_ref.at[0], cot_all.at[own_group], load_sem.at[10])
     cot_load.start()
 
     events_copy.wait()
 
     def project(k):
-        for p in range(3):
-            weight_copy(k, p).wait()
+        pltpu.make_async_copy(w_qkv.at[k], w_qkv.at[k], load_sem.at[k]).wait()
         pre = dot(event_rows[...], w_qkv[k])
         sig = sigmoid(pre)
         act = pre * sig
@@ -262,7 +264,7 @@
         return carry
 
     lax.fori_loop(0, 1, project_keep, 0)
-    pl.semaphore_wait(barrier, 30)
+    pl.semaphore_wait(barrier, 22)
     lax.fori_loop(0, 1, send_kept, 0)
     lax.fori_loop(1, 5, project_send, 0)
     lax.fori_loop(5, 7, project_keep, 0)
@@ -288,7 +290,7 @@
     def gn_copy(k):
         cols = pl.ds(aligned(seq_head(k) * HEAD, HEAD), HEAD)
         return remote(
-            gn_rows.at[:, cols], recv_gn.at[back(k)], gn_ss.at[k], gn_rs.at[back(k)], seq_peer(k)
+            gn_rows.at[:, cols], recv_gn.at[back(k)], gn_ss, gn_rs.at[back(k)], seq_peer(k)
         )
 
     def send_gn(k, carry):
@@ -301,7 +303,7 @@
 
     def cot_copy(k):
         return remote(
-            cot_all.at[own_group], cot_all.at[own_group], cot_ss.at[k], cot_rs.at[2 - k], y_peer(k)
+            cot_all.at[own_group], cot_all.at[own_group], cot_ss, cot_rs, y_peer(k)
         )
 
     def send_cot(k, carry):
@@ -335,9 +337,10 @@
             leading = lax.clz(column_stamp - stamps[:, pl.ds(j * HEAD, HEAD)])
             visible = (key_pos >= first) & (key_pos <= row_pos)
             bias[where] = jnp.where(
-                visible, jnp.take_along_axis(table, leading, axis=1), HIDDEN
+                visible, pick_lane(table, leading), HIDDEN
             )
-            bucket[where] = jnp.minimum(32 - leading, BUCKETS - 1)
+            if j <= i:
+                bucket[where] = jnp.minimum(32 - leading, BUCKETS - 1)
 
     def halves(block):
         return (
@@ -394,6 +397,7 @@
         g = gn_head[rows, :].astype(F32)
         mean = jnp.mean(a, axis=1, keepdims=True)
         off = a - mean
+        centred_head[rows, :] = off.astype(BF16)
         return (
             mean,
             jnp.sum(off * off, axis=1, keepdims=True),
@@ -409,7 +413,7 @@
 
     def stat_copy(k):
         return remote(
-            stat_send, stat_recv.at[back(k)], stat_ss.at[k], stat_rs.at[back(k)], seq_peer(k)
+            stat_send, stat_recv.at[back(k)], stat_ss, stat_rs, seq_peer(k)
         )
 
     def send_stat(k, carry):
@@ -418,15 +422,39 @@
 
     lax.fori_loop(0, 7, send_stat, 0)
     stat_recv[7] = stat_send[...]
+
+    def centred_copy(k):
+        return remote(
+            send_centred.at[k],
+            recv_centred.at[back(k)],
+            centred_ss,
+            centred_rs.at[back(k)],
+            seq_peer(k),
+        )
+
+    def pick_centred(k, target):
+        low, high = halves(seq_head(k))
+        target[k, :HALF] = centred_head[low, :]
+        target[k, HALF:] = centred_head[high, :]
+
+    def send_norm(k, carry):
+        pick_centred(k, send_centred)
+        centred_copy(k).start()
+        return carry
+
+    lax.fori_loop(0, 7, send_norm, 0)
+    pick_centred(7, recv_centred)
+
     for i in range(8):
         rows = pl.ds(i * HEAD, HEAD)
         query_t[:, rows] = jnp.transpose(query[rows, :])
 
-    def take_stat(j, carry):
-        stat_copy(back(j)).wait_recv()
-        return carry
-
-    lax.fori_loop(0, 7, take_stat, 0)
+    wait_bytes(stat_recv.at[:7], stat_rs)
+
+    wait_bytes(cot_all.at[:3], cot_rs)
+    pairs = cot_all.reshape(4, 2, ROWS, WIDTH)
+    cot_core = remote(pairs.at[:, core], pairs.at[:, core], core_ss, core_rs, core_peer)
+    cot_core.start()
 
     for part in range(2):
         rows4 = [[stat_recv[j, part * 4 + n : part * 4 + n + 1, :] for n in range(4)] for j in range(SEQ)]
@@ -435,42 +463,23 @@
         inverse = 1.0 / jnp.sqrt(spread * (1.0 / WIDTH) + NORM_EPS)
         along = sum(r[2] + (r[0] - mu) * r[3] for r in rows4) * inverse * (1.0 / WIDTH)
         level = sum(r[3] for r in rows4) * (1.0 / WIDTH)
+        columns = jnp.concatenate(
+            [mu, inverse, along, level] + [r[0] - mu for r in rows4] + [jnp.zeros_like(mu)] * 4, axis=0
+        )
         for i in range(4):
             at = slice(i * HEAD, (i + 1) * HEAD)
-            tile = jnp.where(
-                sub == 0,
-                mu[:, at],
-                jnp.where(sub == 1, inverse[:, at], jnp.where(sub == 2, along[:, at], level[:, at])),
+            tile = jnp.transpose(
+                jnp.concatenate([columns[:, at], jnp.zeros((HEAD - 16, HEAD), F32)], axis=0)
             )
-            tile = jnp.transpose(tile)
-            rows = pl.ds((part * 4 + i) * HEAD, HEAD)
-            normed = (attn[rows, :] - tile[:, 0:1]) * tile[:, 1:2]
-            normed_head[rows, :] = normed.astype(BF16)
-            grad_attn[rows, :] = (
-                (gn_head[rows, :].astype(F32) - tile[:, 3:4] - normed * tile[:, 2:3]) * tile[:, 1:2]
-            ).astype(BF16)
-
-    def normed_copy(k):
-        return remote(
-            send_normed.at[k],
-            recv_normed.at[back(k)],
-            normed_ss.at[k],
-            normed_rs.at[back(k)],
-            seq_peer(k),
-        )
-
-    def pick_normed(k, target):
-        low, high = halves(seq_head(k))
-        target[k, :HALF] = normed_head[low, :]
-        target[k, HALF:] = normed_head[high, :]
-
-    def send_norm(k, carry):
-        pick_normed(k, send_normed)
-        normed_copy(k).start()
-        return carry
-
-    lax.fori_loop(0, 7, send_norm, 0)
-    pick_normed(7, recv_normed)
+            row_stats[pl.ds((part * 4 + i) * HEAD, HEAD), :] = tile
+
+    for i in range(8):
+        rows = pl.ds(i * HEAD, HEAD)
+        tile = row_stats[rows, :]
+        normed = (attn[rows, :] - tile[:, 0:1]) * tile[:, 1:2]
+        grad_attn[rows, :] = (
+            (gn_head[rows, :].astype(F32) - tile[:, 3:4] - normed * tile[:, 2:3]) * tile[:, 1:2]
+        ).astype(BF16)
 
     for i in range(8):
         rows = pl.ds(i * HEAD, HEAD)
@@ -496,7 +505,7 @@
 
     def dqkv_copy(k):
         return remote(
-            send_dqkv.at[k], recv_dqkv.at[back(k)], dqkv_ss.at[k], dqkv_rs.at[back(k)], seq_peer(k)
+            send_dqkv.at[k], recv_dqkv.at[back(k)], dqkv_ss, dqkv_rs.at[back(k)], seq_peer(k)
         )
 
     def pick_dqkv(k, target):
@@ -509,70 +518,72 @@
         dqkv_copy(k).start()
         return carry
 
-    lax.fori_loop(0, 5, send_grad, 0)
-    pick_dqkv(5, send_dqkv)
-    pick_dqkv(6, send_dqkv)
+    lax.fori_loop(0, 7, send_grad, 0)
     pick_dqkv(7, recv_dqkv)
 
-    for k in range(3):
-        cot_copy(k).wait_recv()
-    pairs = cot_all.reshape(4, 2, ROWS, WIDTH)
-    cot_core = remote(pairs.at[:, core], pairs.at[:, core], core_ss, core_rs, core_peer)
-    cot_core.start()
-
+    low, high = halves(seq)
+    own_stats = jnp.concatenate([row_stats[low, :], row_stats[high, :]], axis=0)
+    for j in (7, 0, 1, 2, 3, 4, 5, 6):
+        if j < 7:
+            centred_copy(back(j)).wait_recv()
+        cols = pl.ds(aligned(seq_head(j) * HEAD, HEAD), HEAD)
+        normed = (recv_centred[j].astype(F32) + own_stats[:, 4 + j : 5 + j]) * own_stats[:, 1:2]
+        mixed[:, cols] = (normed * gate_rows[:, cols].astype(F32)).astype(BF16)
+        gp_gate[:, cols] = (grad_mixed[:, cols] * normed * slope_gate[:, cols]).astype(BF16)
+
+    def mixed_block(k):
+        return pl.ds(aligned(group_index(k) * HEAD, HEAD), HEAD)
+
+    def mixed_copy(k):
+        return remote(
+            mixed.at[:, mixed_block(k)],
+            mixed_all.at[own_group],
+            mixed_ss,
+            mixed_rs,
+            group_peer(k),
+        )
+
+    def send_mixed(k, carry):
+        mixed_copy(k).start()
+        return carry
+
+    lax.fori_loop(0, 7, send_mixed, 0)
+    mixed_all[own_group] = mixed[:, mixed_block(7)]
     def bucket_sums(i, sums):
         def add_rows(r, sums):
-            rows = pl.ds(aligned(i * STEP + r * 8, 8), 8)
-            for j in range(2 * (i + 1)):
-                cols = pl.ds(j * HEAD, HEAD)
-                ds = slope[rows, cols]
-                which = bucket[rows, cols]
-                sums = tuple(
-                    total + jnp.where(which == b, ds, 0.0) for b, total in enumerate(sums)
-                )
+            for block in (i, 7 - i):
+                rows = pl.ds(aligned(block * HEAD + r * 8, 8), 8)
+                for j in range(block + 1):
+                    cols = pl.ds(j * HEAD, HEAD)
+                    ds = slope[rows, cols]
+                    which = bucket[rows, cols]
+                    sums = tuple(
+                        total + jnp.where(which == b, ds, 0.0) for b, total in enumerate(sums)
+                    )
             return sums
 
-        return lax.fori_loop(0, STEP // 8, add_rows, sums)
+        return lax.fori_loop(0, HEAD // 8, add_rows, sums)
 
     sums = tuple(jnp.zeros((8, HEAD), F32) for _ in range(BUCKETS))
-    for i in (0, 3):
+    for i in range(4):
         sums = bucket_sums(i, sums)
-    dqkv_copy(0).wait_send()
-    dqkv_copy(5).start()
-    def rows_of_head(j):
-        cols = pl.ds(aligned(seq_head(j) * HEAD, HEAD), HEAD)
-        normed = recv_normed[j].astype(F32)
-        mixed[:, cols] = (normed * gate_rows[:, cols].astype(F32)).astype(BF16)
-        gp_gate[:, cols] = (grad_mixed[:, cols] * normed * slope_gate[:, cols]).astype(BF16)
-
-    def take_normed(j, carry):
-        normed_copy(back(j)).wait_recv()
-        rows_of_head(j)
-        return carry
-
-    rows_of_head(7)
-    lax.fori_loop(0, 7, take_normed, 0)
-
-    def mixed_block(k):
-        return pl.ds(aligned(group_index(k) * HEAD, HEAD), HEAD)
-
-    def mixed_copy(k):
-        return remote(
-            mixed.at[:, mixed_block(k)],
-            mixed_all.at[own_group],
-            mixed_ss.at[k],
-            mixed_rs.at[6 - k],
-            group_peer(k),
-        )
-
-    def send_mixed(k, carry):
-        mixed_copy(k).start()
-        return carry
-
-    lax.fori_loop(0, 7, send_mixed, 0)
-    mixed_all[own_group] = mixed[:, mixed_block(7)]
-    dqkv_copy(1).wait_send()
-    dqkv_copy(6).start()
+    sums = [jnp.sum(total, axis=0, keepdims=True) for total in sums]
+    sums = jnp.transpose(
+        jnp.concatenate(sums + [jnp.zeros((HEAD - BUCKETS, HEAD), F32)], axis=0)
+    )
+    hist_recv[own_piece] = jnp.sum(sums.reshape(HEAD // 8, 8, HEAD), axis=0)
+
+    def hist_copy(k):
+        return remote(
+            hist_recv.at[own_piece], hist_recv.at[own_piece], hist_ss, hist_rs, piece_peer(k)
+        )
+
+    def send_hist(k, carry):
+        hist_copy(k).start()
+        return carry
+
+    lax.fori_loop(0, 15, send_hist, 0)
+
     for c in range(4):
         cols = pl.ds(c * STEP, STEP)
         layer_out_rows[:, cols] = dot(mixed[...], w_out[:, cols]).astype(BF16)
@@ -580,23 +591,7 @@
     layer_out_copy = pltpu.make_async_copy(layer_out_rows, layer_out_ref.at[0], store_sem.at[0])
     layer_out_copy.start()
 
-    for i in (1, 2):
-        sums = bucket_sums(i, sums)
-    hist[...] = jnp.zeros((24, HEAD), F32)
-    for b in range(BUCKETS):
-        hist[b : b + 1, :] = jnp.sum(sums[b], axis=0, keepdims=True)
-
-    def hist_copy(k):
-        return remote(hist, hist_recv.at[14 - k], hist_ss.at[k], hist_rs.at[14 - k], dp_peer(k))
-
-    def send_hist(k, carry):
-        hist_copy(k).start()
-        return carry
-
-    lax.fori_loop(0, 15, send_hist, 0)
-
-    for k in range(7):
-        mixed_copy(k).wait_recv()
+    wait_bytes(mixed_all.at[:7], mixed_rs)
     cot_core.wait_recv()
     for g in range(8):
         mixed_t[:, g * ROWS : (g + 1) * ROWS] = jnp.transpose(mixed_all[g])
@@ -616,8 +611,8 @@
         return remote(
             piece.at[piece_index(k)],
             piece_recv.at[14 - k],
-            piece_ss.at[k],
-            piece_rs.at[14 - k],
+            piece_ss,
+            piece_rs,
             piece_peer(k),
         )
 
@@ -639,90 +634,72 @@
         return carry
 
     add_head(7)
-    lax.fori_loop(0, 7, take_dqkv, 0)
+    lax.fori_loop(0, 4, take_dqkv, 0)
+    wait_bytes(hist_recv.at[:15], hist_rs)
+    heads = jnp.sum(hist_recv[:SEQ] + hist_recv[SEQ:], axis=1) * norm_scale
+    hist_all[own_group] = heads
+
+    def all_copy(k):
+        return remote(
+            hist_all.at[own_group], hist_all.at[own_group], all_ss, all_rs, group_peer(k)
+        )
+
+    def send_all(k, carry):
+        all_copy(k).start()
+        return carry
+
+    lax.fori_loop(0, 7, send_all, 0)
+
+    def take_piece(k, total):
+        return total + piece_recv[k].astype(F32)
+
+    wait_bytes(piece_recv, piece_rs)
+    total = lax.fori_loop(0, 15, take_piece, piece[own_piece].astype(F32)) * norm_scale
+    final_send[...] = total.reshape(8, 8, HEAD)
+
+    def final_copy(k):
+        return remote(
+            final_send.at[group_index(k)],
+            final_recv.at[own_group],
+            final_ss,
+            final_rs,
+            group_peer(k),
+        )
+
+    def send_final(k, carry):
+        final_copy(k).start()
+        return carry
+
+    lax.fori_loop(0, 7, send_final, 0)
+    final_recv[own_group] = final_send[own_group]
+
+    lax.fori_loop(4, 7, take_dqkv, 0)
     input_grad_rows[...] = ig_acc[...].astype(BF16)
     input_grad_copy = pltpu.make_async_copy(
         input_grad_rows, input_grad_ref.at[0], store_sem.at[1]
     )
     input_grad_copy.start()
 
-    def take_hist(k, total):
-        hist_copy(14 - k).wait_recv()
-        return total + hist_recv[k]
-
-    hist_sum[...] = lax.fori_loop(0, 15, take_hist, hist[...]) * norm_scale
-
-    def all_copy(k):
-        return remote(hist_sum, hist_all.at[back(k)], all_ss.at[k], all_rs.at[back(k)], seq_peer(k))
-
-    def send_all(k, carry):
-        all_copy(k).start()
-        return carry
-
-    lax.fori_loop(0, 7, send_all, 0)
-
-    def take_piece(k, total):
-        piece_copy(14 - k).wait_recv()
-        return total + piece_recv[k].astype(F32)
-
-    total = lax.fori_loop(0, 15, take_piece, piece[own_piece].astype(F32)) * norm_scale
-    final_send[...] = total.reshape(8, 8, HEAD)
-
-    def final_copy(k):
-        return remote(
-            final_send.at[group_index(k)],
-            final_recv.at[own_group],
-            final_ss.at[k],
-            final_rs.at[6 - k],
-            group_peer(k),
-        )
-
-    def send_final(k, carry):
-        final_copy(k).start()
-        return carry
-
-    lax.fori_loop(0, 7, send_final, 0)
-    final_recv[own_group] = final_send[own_group]
-
-    def head_column(j, table):
-        column = jnp.sum(hist_all[j], axis=1, keepdims=True)
-        return jnp.where(lane[:24] == seq_head(j), column, table)
-
-    hist_all[7] = hist_sum[...]
-
-    def take_all(j, table):
-        all_copy(back(j)).wait_recv()
-        return head_column(j, table)
-
-    table = head_column(7, jnp.zeros((24, HEAD), F32))
-    table = lax.fori_loop(0, 7, take_all, table)
-    table = jnp.transpose(jnp.concatenate([table, jnp.zeros((HEAD - 24, HEAD), F32)], axis=0))
-    bias_grad_ref[...] = table[:8, :BUCKETS]
-
-    for k in range(7):
-        final_copy(k).wait_recv()
+    wait_bytes(hist_all.at[:7], all_rs)
+    bias_grad_ref[...] = jnp.sum(hist_all[...], axis=0)[:, :BUCKETS]
+
+    wait_bytes(final_recv.at[:7], final_rs)
     for g in range(8):
         out_grad_ref[:, g * HEAD : (g + 1) * HEAD] = final_recv[g]
 
-    def sent_seq(k, carry):
-        for copy in (gn_copy, stat_copy, normed_copy, mixed_copy, all_copy, final_copy):
-            copy(k).wait_send()
-        return carry
-
-    def sent_many(k, carry):
-        piece_copy(k).wait_send()
-        hist_copy(k).wait_send()
-        return carry
-
-    lax.fori_loop(0, 7, sent_seq, 0)
-    lax.fori_loop(0, 15, sent_many, 0)
-    for k in range(3):
-        cot_copy(k).wait_send()
+    wait_bytes(recv_gn.at[:7], gn_ss)
+    wait_bytes(stat_recv.at[:7], stat_ss)
+    wait_bytes(recv_centred.at[:7], centred_ss)
+    wait_bytes(mixed_all.at[:7], mixed_ss)
+    wait_bytes(hist_all.at[:7], all_ss)
+    wait_bytes(final_recv.at[:7], final_ss)
+    wait_bytes(piece_recv, piece_ss)
+    wait_bytes(hist_recv.at[:15], hist_ss)
+    wait_bytes(cot_all.at[:3], cot_ss)
     cot_core.wait_send()
     for k in range(4, 7):
         qkv_copy(k).wait_send()
-    for k in range(2, 7):
-        dqkv_copy(k).wait_send()
+    wait_bytes(recv_dqkv.at[:7], dqkv_ss)
     layer_out_copy.wait()
     input_grad_copy.wait()
 
@@ -765,6 +742,7 @@
         vmem((8, LEN // 2), F32),
         vmem((SEQ, 8, LEN // 2), F32),
         vmem((LEN, HEAD), BF16),
+        vmem((LEN, HEAD), F32),
         vmem((LEN, HEAD), BF16),
         vmem((HEAD, LEN), BF16),
         vmem((HEAD, LEN), BF16),
@@ -784,10 +762,8 @@
         vmem((15, HALF, HEAD), BF16),
         vmem((8, 8, HEAD), F32),
         vmem((8, 8, HEAD), F32),
-        vmem((24, HEAD), F32),
-        vmem((15, 24, HEAD), F32),
-        vmem((24, HEAD), F32),
-        vmem((SEQ, 24, HEAD), F32),
+        vmem((16, 8, HEAD), F32),
+        vmem((8, 8, HEAD), F32),
         pltpu.SMEM((SEQ, BUCKETS), F32),
         pltpu.SMEM((1, 4), jnp.int32),
         vmem((1, LEN), jnp.int32),
@@ -795,31 +771,31 @@
         vmem((ROWS, WIDTH), BF16),
         dma((2,)),
         dma((3,)),
-        dma((28,)),
+        dma((12,)),
         dma((7,)),
         dma((7,)),
+        dma,
         dma((7,)),
+        dma,
+        dma,
+        dma,
         dma((7,)),
+        dma,
         dma((7,)),
-        dma((7,)),
-        dma((7,)),
-        dma((7,)),
-        dma((7,)),
-        dma((7,)),
-        dma((3,)),
-        dma((3,)),
-        dma,
-        dma,
-        dma((7,)),
-        dma((7,)),
-        dma((7,)),
-        dma((7,)),
-        dma((15,)),
-        dma((15,)),
-        dma((15,)),
-        dma((15,)),
-        dma((7,)),
-        dma((7,)),
+        dma,
+        dma,
+        dma,
+        dma,
+        dma,
+        dma,
+        dma,
+        dma,
+        dma,
+        dma,
+        dma,
+        dma,
+        dma,
+        dma,
     ]
     hbm = pl.BlockSpec(memory_space=pl.ANY)
     local = pl.BlockSpec(memory_space=pltpu.VMEM)

time: 60 us -> 53.9 us (0.90)
  Pallas kernels: 59.2 us -> 53.1 us
    pallas_call x1, Pallas kernels: 57.4 us -> 51.2 us  [body(): pl.pallas_call(kernel, out_shape=shapes, in_specs=[hbm] * 7, out_specs=(h...]
where the time goes in v3:
time: 53.9 us; the launch traced here: 53.7 us
  Pallas kernels  53.1 us (99%)
  between operations  0.64 us (1%)
    pallas_call x1, Pallas kernels, body(): pl.pallas_call(kernel, out_shape=shapes, in_specs=[hbm] * 7, out_specs=(h...  51.2 us
    pallas_call x1, Pallas kernels, body(): pl.pallas_call(finish, out_shape=shapes, in_specs=[local] * 4, out_specs=...  1.85 us

profile of v3, /device:TPU:1, one launch (start us, length us, event | category | flops | bytes accessed | tf_op | source)
XLA Modules:
  0.0 53.7 jit_solution(7107365395109775430)
XLA Ops:
  0.6 51.2 %shard_map.102 = (bf16[1,128,1024]{2,1,0:T(8,128)(2,1)}, bf16[1,128,1024]{2,1,0:T(8,128)(2,1)}, f32[8,1024]{1,0:T(8,128)}, f32[8,18]{1,0:T(8,128)}) custom-call(bf16[1,128,1024]{2,1,0:T(8,128)(2,1)} %events_ref.1, bf16[1024,4096]{1,0:T(8,128)(2,1)} %in_weight_ref.1, bf16[1024,1024]{1,0:T(8,128)(2,1)} %out_weight_ref.1, f32[8,18]{1,0:T(8,128)} %bitcast.3, ...), custom_call_target="tpu_custom_call" | custom-call | tf_op jit(solution)/shard_map/pallas_call | solution.py:808
  51.9 1.8 %shard_map.103 = (bf16[1,128,1024]{2,1,0:T(8,128)(2,1)}, bf16[1,128,1024]{2,1,0:T(8,128)(2,1)}, f32[8,1024]{1,0:T(8,128)}, f32[8,18]{1,0:T(8,128)}) custom-call(bf16[1,128,1024]{2,1,0:T(8,128)(2,1)} %get-tuple-element.12.refs_0_, bf16[1,128,1024]{2,1,0:T(8,128)(2,1)} %get-tuple-element.13.refs_1_, f32[8,1024]{1,0:T(8,128)} %get-tuple-element.14.refs_2_, ...), custom_call_target="tpu_custom_call" | custom-call | tf_op jit(solution)/shard_map/pallas_call | solution.py:818

commit v4 on v3

--- a/solution.py
+++ b/solution.py
@@ -22,6 +22,7 @@
 HEAD = 128
 BUCKETS = 18
 STEP = 256
+PACKS = 3
 
 
 def dot(left, right):
@@ -34,6 +35,10 @@
 
 def sigmoid(values):
     return 0.5 * jnp.tanh(0.5 * values) + 0.5
+
+
+def pack_groups(p):
+    return [(a, 7 * p + a) for a in range(7) if 7 * p + a < 16]
 
 
 def pick_lane(values, lanes):
@@ -72,7 +77,8 @@
     value,
     gn_head,
     bias,
-    bucket,
+    limit,
+    last_key,
     slope,
     probs,
     dscores,
@@ -319,12 +325,21 @@
     for b in range(BUCKETS):
         table = jnp.where(table_bucket == b, rab[seq, b], table)
     table = jnp.broadcast_to(table[:1], (HEAD, HEAD))
+    group = sum((lane[:8] >= BUCKETS * a).astype(jnp.int32) for a in range(1, 8))
+    which = lane - BUCKETS * sum((lane >= BUCKETS * a).astype(jnp.int32) for a in range(1, 8))
+    power = jnp.left_shift(1, jnp.minimum(which, BUCKETS - 2))
     end_0 = lengths[0, 0]
     end_1 = end_0 + lengths[0, 1]
     end_2 = end_1 + lengths[0, 2]
     for i in range(8):
         row_stamp = stamps[:, pl.ds(i * HEAD, HEAD)].astype(F32)
         column_stamp = jnp.transpose(jnp.broadcast_to(row_stamp, (HEAD, HEAD))).astype(jnp.int32)
+        limits = jnp.where(which < BUCKETS - 1, column_stamp - power, 1 << 30)
+        for p in range(PACKS):
+            packed = jnp.full((8, HEAD), -1, jnp.int32)
+            for a, g in pack_groups(p):
+                packed = jnp.where(group == a, limits[g * 8 : g * 8 + 8], packed)
+            limit[i, p * 8 : p * 8 + 8, :] = packed
         row_pos = sub + i * HEAD
         first = jnp.where(
             row_pos >= end_2,
@@ -339,8 +354,21 @@
             bias[where] = jnp.where(
                 visible, pick_lane(table, leading), HIDDEN
             )
-            if j <= i:
-                bucket[where] = jnp.minimum(32 - leading, BUCKETS - 1)
+
+    def find_last(i):
+        keys = jnp.concatenate(
+            [
+                jnp.broadcast_to(stamps[:, j * HEAD : (j + 1) * HEAD], (8 * PACKS, HEAD))
+                for j in range(i + 1)
+            ],
+            axis=0,
+        )
+        most = jnp.concatenate([limit[i]] * (i + 1), axis=0)
+        last = jnp.full(most.shape, -1, jnp.int32)
+        for step in (64, 32, 16, 8, 4, 2, 1, 1):
+            later = last + step
+            last = jnp.where(pick_lane(keys, later) <= most, later, last)
+        last_key[i, : 8 * PACKS * (i + 1), :] = last
 
     def halves(block):
         return (
@@ -364,6 +392,8 @@
     qkv_copy(3).wait_send()
     lax.fori_loop(0, 7, send_gn, 0)
     lax.fori_loop(0, 3, send_cot, 0)
+    for i in range(8):
+        find_last(i)
     lax.fori_loop(0, 7, take_qkv, 0)
 
     def place_gn(j):
@@ -489,7 +519,6 @@
         for j in range(i + 1):
             cols = pl.ds(j * STEP, STEP)
             ds = dot_t(grad_attn[rows, :], value[cols, :]) * slope[rows, cols]
-            slope[rows, cols] = ds
             dscores[rows, cols] = ds.astype(BF16)
         seen = (i + 1) * STEP
         dqkv_head[rows, HEAD : 2 * HEAD] = (
@@ -549,29 +578,22 @@
 
     lax.fori_loop(0, 7, send_mixed, 0)
     mixed_all[own_group] = mixed[:, mixed_block(7)]
-    def bucket_sums(i, sums):
-        def add_rows(r, sums):
-            for block in (i, 7 - i):
-                rows = pl.ds(aligned(block * HEAD + r * 8, 8), 8)
-                for j in range(block + 1):
-                    cols = pl.ds(j * HEAD, HEAD)
-                    ds = slope[rows, cols]
-                    which = bucket[rows, cols]
-                    sums = tuple(
-                        total + jnp.where(which == b, ds, 0.0) for b, total in enumerate(sums)
+    lower = (sub <= lane).astype(F32).astype(BF16)
+    sums = jnp.zeros((8, HEAD), F32)
+    for i in range(8):
+        rows = pl.ds(i * HEAD, HEAD)
+        for j in range(i + 1):
+            running = dot(dscores[rows, pl.ds(j * HEAD, HEAD)], lower)
+            for p in range(PACKS):
+                last = last_key[i, (j * PACKS + p) * 8 : (j * PACKS + p) * 8 + 8, :]
+                lanes = jnp.maximum(last, 0)
+                at_limit = jnp.zeros((8, HEAD), F32)
+                for a, g in pack_groups(p):
+                    at_limit = jnp.where(
+                        group == a, pick_lane(running[g * 8 : g * 8 + 8], lanes), at_limit
                     )
-            return sums
-
-        return lax.fori_loop(0, HEAD // 8, add_rows, sums)
-
-    sums = tuple(jnp.zeros((8, HEAD), F32) for _ in range(BUCKETS))
-    for i in range(4):
-        sums = bucket_sums(i, sums)
-    sums = [jnp.sum(total, axis=0, keepdims=True) for total in sums]
-    sums = jnp.transpose(
-        jnp.concatenate(sums + [jnp.zeros((HEAD - BUCKETS, HEAD), F32)], axis=0)
-    )
-    hist_recv[own_piece] = jnp.sum(sums.reshape(HEAD // 8, 8, HEAD), axis=0)
+                sums = sums + jnp.where(last >= 0, at_limit, 0.0)
+    hist_recv[own_piece] = sums
 
     def hist_copy(k):
         return remote(
@@ -583,13 +605,6 @@
         return carry
 
     lax.fori_loop(0, 15, send_hist, 0)
-
-    for c in range(4):
-        cols = pl.ds(c * STEP, STEP)
-        layer_out_rows[:, cols] = dot(mixed[...], w_out[:, cols]).astype(BF16)
-        ig_acc[:, cols] = dot_t(gp_gate[...], w_gate[cols, :])
-    layer_out_copy = pltpu.make_async_copy(layer_out_rows, layer_out_ref.at[0], store_sem.at[0])
-    layer_out_copy.start()
 
     wait_bytes(mixed_all.at[:7], mixed_rs)
     cot_core.wait_recv()
@@ -622,6 +637,13 @@
 
     lax.fori_loop(0, 15, send_piece, 0)
 
+    for c in range(4):
+        cols = pl.ds(c * STEP, STEP)
+        layer_out_rows[:, cols] = dot(mixed[...], w_out[:, cols]).astype(BF16)
+        ig_acc[:, cols] = dot_t(gp_gate[...], w_gate[cols, :])
+    layer_out_copy = pltpu.make_async_copy(layer_out_rows, layer_out_ref.at[0], store_sem.at[0])
+    layer_out_copy.start()
+
     def add_head(j):
         grad_pre = (recv_dqkv[j].astype(F32) * slope_qkv[j]).astype(BF16)
         for c in range(4):
@@ -681,7 +703,14 @@
     input_grad_copy.start()
 
     wait_bytes(hist_all.at[:7], all_rs)
-    bias_grad_ref[...] = jnp.sum(hist_all[...], axis=0)[:, :BUCKETS]
+    packed = jnp.sum(hist_all[...], axis=0)
+    reached = packed
+    for a in range(1, 7):
+        reached = reached + pltpu.roll(packed, HEAD - BUCKETS * a, 1)
+    every = reached[:, BUCKETS - 1 : BUCKETS]
+    reached = jnp.where(lane[:8] == BUCKETS - 1, 0.0, reached)
+    before = jnp.where(lane[:8] == 0, every, pltpu.roll(reached, 1, 1))
+    bias_grad_ref[...] = (before - reached)[:, :BUCKETS]
 
     wait_bytes(final_recv.at[:7], final_rs)
     for g in range(8):
@@ -734,7 +763,8 @@
         vmem((LEN, HEAD), BF16),
         vmem((LEN, HEAD), BF16),
         vmem((LEN, LEN), F32),
-        vmem((LEN, LEN), jnp.int32),
+        vmem((8, 8 * PACKS, HEAD), jnp.int32),
+        vmem((8, 64 * PACKS, HEAD), jnp.int32),
         vmem((LEN, LEN), F32),
         vmem((LEN, LEN), BF16),
         vmem((LEN, LEN), BF16),

time: 53.9 us -> 53 us (0.983)
  Pallas kernels: 53.1 us -> 52.2 us
    pallas_call x1, Pallas kernels: 51.2 us -> 50.4 us  [body(): pl.pallas_call(kernel, out_shape=shapes, in_specs=[hbm] * 7, out_specs=(h...]
where the time goes in v4:
time: 53 us; the launch traced here: 52.9 us
  Pallas kernels  52.2 us (98%)
  between operations  0.64 us (1%)
    pallas_call x1, Pallas kernels, body(): pl.pallas_call(kernel, out_shape=shapes, in_specs=[hbm] * 7, out_specs=(h...  50.4 us
    pallas_call x1, Pallas kernels, body(): pl.pallas_call(finish, out_shape=shapes, in_specs=[local] * 4, out_specs=...  1.85 us

profile of v4, /device:TPU:1, one launch (start us, length us, event | category | flops | bytes accessed | tf_op | source)
XLA Modules:
  0.0 52.9 jit_solution(17148750415294039519)
XLA Ops:
  0.6 50.4 %shard_map.102 = (bf16[1,128,1024]{2,1,0:T(8,128)(2,1)}, bf16[1,128,1024]{2,1,0:T(8,128)(2,1)}, f32[8,1024]{1,0:T(8,128)}, f32[8,18]{1,0:T(8,128)}) custom-call(bf16[1,128,1024]{2,1,0:T(8,128)(2,1)} %events_ref.1, bf16[1024,4096]{1,0:T(8,128)(2,1)} %in_weight_ref.1, bf16[1024,1024]{1,0:T(8,128)(2,1)} %out_weight_ref.1, f32[8,18]{1,0:T(8,128)} %bitcast.3, ...), custom_call_target="tpu_custom_call" | custom-call | tf_op jit(solution)/shard_map/pallas_call | solution.py:838
  51.0 1.8 %shard_map.103 = (bf16[1,128,1024]{2,1,0:T(8,128)(2,1)}, bf16[1,128,1024]{2,1,0:T(8,128)(2,1)}, f32[8,1024]{1,0:T(8,128)}, f32[8,18]{1,0:T(8,128)}) custom-call(bf16[1,128,1024]{2,1,0:T(8,128)(2,1)} %get-tuple-element.12.refs_0_, bf16[1,128,1024]{2,1,0:T(8,128)(2,1)} %get-tuple-element.13.refs_1_, f32[8,1024]{1,0:T(8,128)} %get-tuple-element.14.refs_2_, ...), custom_call_target="tpu_custom_call" | custom-call | tf_op jit(solution)/shard_map/pallas_call | solution.py:848

commit v5 on v4

--- a/solution.py
+++ b/solution.py
@@ -126,6 +126,8 @@
     centred_rs,
     dqkv_ss,
     dqkv_rs,
+    dv_ss,
+    dv_rs,
     cot_ss,
     cot_rs,
     core_ss,
@@ -199,28 +201,6 @@
     events_copy = pltpu.make_async_copy(events_ref.at[0], event_rows, load_sem.at[11])
     events_copy.start()
 
-    small_copies = [
-        pltpu.make_async_copy(source, target, small_sem.at[n])
-        for n, (source, target) in enumerate(
-            ((rab_ref, rab), (lengths_ref, lengths), (stamps_ref, stamps))
-        )
-    ]
-    for copy in small_copies:
-        copy.start()
-
-    barrier = pltpu.get_barrier_semaphore()
-
-    def greet_piece(k, carry):
-        pl.semaphore_signal(barrier, inc=1, device_id=piece_peer(k), device_id_type=MESH)
-        return carry
-
-    def greet_group(k, carry):
-        pl.semaphore_signal(barrier, inc=1, device_id=group_peer(k), device_id_type=MESH)
-        return carry
-
-    lax.fori_loop(0, 15, greet_piece, 0)
-    lax.fori_loop(0, 7, greet_group, 0)
-
     def weight_copy(k, p):
         head = seq_head(k)
         return pltpu.make_async_copy(
@@ -229,7 +209,32 @@
             load_sem.at[k],
         )
 
-    for k in range(SEQ):
+    for p in range(3):
+        weight_copy(0, p).start()
+
+    small_copies = [
+        pltpu.make_async_copy(source, target, small_sem.at[n])
+        for n, (source, target) in enumerate(
+            ((rab_ref, rab), (lengths_ref, lengths), (stamps_ref, stamps))
+        )
+    ]
+    for copy in small_copies:
+        copy.start()
+
+    barrier = pltpu.get_barrier_semaphore()
+
+    def greet_piece(k, carry):
+        pl.semaphore_signal(barrier, inc=1, device_id=piece_peer(k), device_id_type=MESH)
+        return carry
+
+    def greet_group(k, carry):
+        pl.semaphore_signal(barrier, inc=1, device_id=group_peer(k), device_id_type=MESH)
+        return carry
+
+    lax.fori_loop(0, 15, greet_piece, 0)
+    lax.fori_loop(0, 7, greet_group, 0)
+
+    for k in range(1, SEQ):
         for p in range(3):
             weight_copy(k, p).start()
     out_weight_copy = pltpu.make_async_copy(out_weight_ref, w_out, load_sem.at[8])
@@ -296,7 +301,7 @@
     def gn_copy(k):
         cols = pl.ds(aligned(seq_head(k) * HEAD, HEAD), HEAD)
         return remote(
-            gn_rows.at[:, cols], recv_gn.at[back(k)], gn_ss, gn_rs.at[back(k)], seq_peer(k)
+            gn_rows.at[:, cols], recv_gn.at[back(k)], gn_ss, gn_rs, seq_peer(k)
         )
 
     def send_gn(k, carry):
@@ -402,7 +407,6 @@
         gn_head[high, :] = recv_gn[j, HALF:]
 
     def take_gn(j, carry):
-        gn_copy(back(j)).wait_recv()
         place_gn(j)
         return carry
 
@@ -419,7 +423,10 @@
         attn[rows, :] = dot(probs[rows, :seen], value[:seen, :])
 
     place_gn(7)
+    wait_bytes(recv_gn.at[:7], gn_rs)
     lax.fori_loop(0, 7, take_gn, 0)
+
+    ones = jnp.ones((HEAD, HEAD), BF16)
 
     def column_stats(i):
         rows = pl.ds(i * HEAD, HEAD)
@@ -431,8 +438,8 @@
         return (
             mean,
             jnp.sum(off * off, axis=1, keepdims=True),
-            jnp.sum(g * off, axis=1, keepdims=True),
-            jnp.sum(g, axis=1, keepdims=True),
+            dot((g * off).astype(BF16), ones),
+            dot(gn_head[rows, :], ones),
         )
 
     for i in range(4):
@@ -458,7 +465,7 @@
             send_centred.at[k],
             recv_centred.at[back(k)],
             centred_ss,
-            centred_rs.at[back(k)],
+            centred_rs,
             seq_peer(k),
         )
 
@@ -514,6 +521,33 @@
     for i in range(8):
         rows = pl.ds(i * HEAD, HEAD)
         grad_attn_t[:, rows] = jnp.transpose(grad_attn[rows, :])
+    for j in range(4):
+        cols = pl.ds(j * STEP, STEP)
+        rest = slice(j * STEP, LEN)
+        grad_value = dot(grad_attn_t[:, rest], probs[rest, cols])
+        dqkv_head[cols, 0:HEAD] = jnp.transpose(grad_value).astype(BF16)
+
+    def dv_copy(k):
+        return remote(
+            send_dqkv.at[k, :, pl.ds(0, HEAD)],
+            recv_dqkv.at[back(k), :, pl.ds(0, HEAD)],
+            dv_ss,
+            dv_rs,
+            seq_peer(k),
+        )
+
+    def pick_dv(k, target):
+        low, high = halves(seq_head(k))
+        target[k, :HALF, :HEAD] = dqkv_head[low, :HEAD]
+        target[k, HALF:, :HEAD] = dqkv_head[high, :HEAD]
+
+    def send_dv(k, carry):
+        pick_dv(k, send_dqkv)
+        dv_copy(k).start()
+        return carry
+
+    lax.fori_loop(0, 7, send_dv, 0)
+    pick_dv(7, recv_dqkv)
     for i in range(4):
         rows = pl.ds(i * STEP, STEP)
         for j in range(i + 1):
@@ -527,20 +561,22 @@
     for j in range(4):
         cols = pl.ds(j * STEP, STEP)
         rest = slice(j * STEP, LEN)
-        grad_value = dot(grad_attn_t[:, rest], probs[rest, cols])
         grad_key = dot(query_t[:, rest], dscores[rest, cols]) * score_scale
-        dqkv_head[cols, 0:HEAD] = jnp.transpose(grad_value).astype(BF16)
         dqkv_head[cols, 2 * HEAD : 3 * HEAD] = jnp.transpose(grad_key).astype(BF16)
 
     def dqkv_copy(k):
         return remote(
-            send_dqkv.at[k], recv_dqkv.at[back(k)], dqkv_ss, dqkv_rs.at[back(k)], seq_peer(k)
+            send_dqkv.at[k, :, pl.ds(HEAD, 2 * HEAD)],
+            recv_dqkv.at[back(k), :, pl.ds(HEAD, 2 * HEAD)],
+            dqkv_ss,
+            dqkv_rs.at[back(k)],
+            seq_peer(k),
         )
 
     def pick_dqkv(k, target):
         low, high = halves(seq_head(k))
-        target[k, :HALF] = dqkv_head[low, :]
-        target[k, HALF:] = dqkv_head[high, :]
+        target[k, :HALF, HEAD:] = dqkv_head[low, HEAD:]
+        target[k, HALF:, HEAD:] = dqkv_head[high, HEAD:]
 
     def send_grad(k, carry):
         pick_dqkv(k, send_dqkv)
@@ -552,13 +588,17 @@
 
     low, high = halves(seq)
     own_stats = jnp.concatenate([row_stats[low, :], row_stats[high, :]], axis=0)
-    for j in (7, 0, 1, 2, 3, 4, 5, 6):
-        if j < 7:
-            centred_copy(back(j)).wait_recv()
-        cols = pl.ds(aligned(seq_head(j) * HEAD, HEAD), HEAD)
-        normed = (recv_centred[j].astype(F32) + own_stats[:, 4 + j : 5 + j]) * own_stats[:, 1:2]
-        mixed[:, cols] = (normed * gate_rows[:, cols].astype(F32)).astype(BF16)
-        gp_gate[:, cols] = (grad_mixed[:, cols] * normed * slope_gate[:, cols]).astype(BF16)
+
+    def own_normed(j):
+        return (recv_centred[j].astype(F32) + own_stats[:, 4 + j : 5 + j]) * own_stats[:, 1:2]
+
+    def own_columns(j):
+        return pl.ds(aligned(seq_head(j) * HEAD, HEAD), HEAD)
+
+    wait_bytes(recv_centred.at[:7], centred_rs)
+    for j in range(SEQ):
+        cols = own_columns(j)
+        mixed[:, cols] = (own_normed(j) * gate_rows[:, cols].astype(F32)).astype(BF16)
 
     def mixed_block(k):
         return pl.ds(aligned(group_index(k) * HEAD, HEAD), HEAD)
@@ -578,6 +618,10 @@
 
     lax.fori_loop(0, 7, send_mixed, 0)
     mixed_all[own_group] = mixed[:, mixed_block(7)]
+    for j in range(SEQ):
+        cols = own_columns(j)
+        gp_gate[:, cols] = (grad_mixed[:, cols] * own_normed(j) * slope_gate[:, cols]).astype(BF16)
+
     lower = (sub <= lane).astype(F32).astype(BF16)
     sums = jnp.zeros((8, HEAD), F32)
     for i in range(8):
@@ -656,6 +700,7 @@
         return carry
 
     add_head(7)
+    wait_bytes(recv_dqkv.at[pl.ds(0, 7), :, pl.ds(0, HEAD)], dv_rs)
     lax.fori_loop(0, 4, take_dqkv, 0)
     wait_bytes(hist_recv.at[:15], hist_rs)
     heads = jnp.sum(hist_recv[:SEQ] + hist_recv[SEQ:], axis=1) * norm_scale
@@ -728,7 +773,8 @@
     cot_core.wait_send()
     for k in range(4, 7):
         qkv_copy(k).wait_send()
-    wait_bytes(recv_dqkv.at[:7], dqkv_ss)
+    wait_bytes(recv_dqkv.at[pl.ds(0, 7), :, pl.ds(HEAD, 2 * HEAD)], dqkv_ss)
+    wait_bytes(recv_dqkv.at[pl.ds(0, 7), :, pl.ds(0, HEAD)], dv_ss)
     layer_out_copy.wait()
     input_grad_copy.wait()
 
@@ -805,13 +851,15 @@
         dma((7,)),
         dma((7,)),
         dma,
+        dma,
+        dma,
+        dma,
+        dma,
+        dma,
+        dma,
         dma((7,)),
         dma,
         dma,
-        dma,
-        dma((7,)),
-        dma,
-        dma((7,)),
         dma,
         dma,
         dma,

time: 53 us -> 52.3 us (0.987)
  Pallas kernels: 52.2 us -> 51.5 us
    pallas_call x1, Pallas kernels: 50.4 us -> 49.7 us  [body(): pl.pallas_call(kernel, out_shape=shapes, in_specs=[hbm] * 7, out_specs=(h...]
where the time goes in v5:
time: 52.3 us; the launch traced here: 52.2 us
  Pallas kernels  51.5 us (98%)
  between operations  0.64 us (1%)
    pallas_call x1, Pallas kernels, body(): pl.pallas_call(kernel, out_shape=shapes, in_specs=[hbm] * 7, out_specs=(h...  49.7 us
    pallas_call x1, Pallas kernels, body(): pl.pallas_call(finish, out_shape=shapes, in_specs=[local] * 4, out_specs=...  1.85 us

profile of v5, /device:TPU:1, one launch (start us, length us, event | category | flops | bytes accessed | tf_op | source)
XLA Modules:
  0.0 52.2 jit_solution(3237527975414932038)
XLA Ops:
  0.6 49.7 %shard_map.102 = (bf16[1,128,1024]{2,1,0:T(8,128)(2,1)}, bf16[1,128,1024]{2,1,0:T(8,128)(2,1)}, f32[8,1024]{1,0:T(8,128)}, f32[8,18]{1,0:T(8,128)}) custom-call(bf16[1,128,1024]{2,1,0:T(8,128)(2,1)} %events_ref.1, bf16[1024,4096]{1,0:T(8,128)(2,1)} %in_weight_ref.1, bf16[1024,1024]{1,0:T(8,128)(2,1)} %out_weight_ref.1, f32[8,18]{1,0:T(8,128)} %bitcast.3, ...), custom_call_target="tpu_custom_call" | custom-call | tf_op jit(solution)/shard_map/pallas_call | solution.py:886
  50.3 1.8 %shard_map.103 = (bf16[1,128,1024]{2,1,0:T(8,128)(2,1)}, bf16[1,128,1024]{2,1,0:T(8,128)(2,1)}, f32[8,1024]{1,0:T(8,128)}, f32[8,18]{1,0:T(8,128)}) custom-call(bf16[1,128,1024]{2,1,0:T(8,128)(2,1)} %get-tuple-element.12.refs_0_, bf16[1,128,1024]{2,1,0:T(8,128)(2,1)} %get-tuple-element.13.refs_1_, f32[8,1024]{1,0:T(8,128)} %get-tuple-element.14.refs_2_, ...), custom_call_target="tpu_custom_call" | custom-call | tf_op jit(solution)/shard_map/pallas_call | solution.py:896

commit v6 on v5

--- a/solution.py
+++ b/solution.py
@@ -128,6 +128,8 @@
     dqkv_rs,
     dv_ss,
     dv_rs,
+    v_ss,
+    v_rs,
     cot_ss,
     cot_rs,
     core_ss,
@@ -258,8 +260,25 @@
 
     def qkv_copy(k):
         return remote(
-            send_qkv.at[k], recv_qkv.at[back(k)], qkv_ss.at[k], qkv_rs.at[back(k)], seq_peer(k)
-        )
+            send_qkv.at[k, :, pl.ds(HEAD, 2 * HEAD)],
+            recv_qkv.at[back(k), :, pl.ds(HEAD, 2 * HEAD)],
+            qkv_ss,
+            qkv_rs.at[back(k)],
+            seq_peer(k),
+        )
+
+    def v_copy(k):
+        return remote(
+            send_qkv.at[k, :, pl.ds(0, HEAD)],
+            recv_qkv.at[back(k), :, pl.ds(0, HEAD)],
+            v_ss,
+            v_rs,
+            seq_peer(k),
+        )
+
+    def send_v(k, carry):
+        v_copy(k).start()
+        return carry
 
     def project_keep(k, carry):
         send_qkv[k] = project(k)
@@ -277,11 +296,9 @@
     lax.fori_loop(0, 1, project_keep, 0)
     pl.semaphore_wait(barrier, 22)
     lax.fori_loop(0, 1, send_kept, 0)
-    lax.fori_loop(1, 5, project_send, 0)
-    lax.fori_loop(5, 7, project_keep, 0)
+    lax.fori_loop(1, 7, project_send, 0)
     recv_qkv[7] = project(7)
-    qkv_copy(0).wait_send()
-    qkv_copy(5).start()
+    lax.fori_loop(0, 7, send_v, 0)
 
     out_weight_copy.wait()
     gate_copy.wait()
@@ -309,8 +326,6 @@
         return carry
 
     recv_gn[7] = gn_rows[:, pl.ds(aligned(seq * HEAD, HEAD), HEAD)]
-    qkv_copy(1).wait_send()
-    qkv_copy(6).start()
 
     def cot_copy(k):
         return remote(
@@ -384,8 +399,8 @@
     def place_qkv(j):
         low, high = halves(seq_head(j))
         for at, rows in ((low, slice(0, HALF)), (high, slice(HALF, ROWS))):
-            for p, target in enumerate((value, query, key)):
-                target[at, :] = recv_qkv[j, rows, p * HEAD : (p + 1) * HEAD]
+            query[at, :] = recv_qkv[j, rows, HEAD : 2 * HEAD]
+            key[at, :] = recv_qkv[j, rows, 2 * HEAD :]
 
     def take_qkv(j, carry):
         qkv_copy(back(j)).wait_recv()
@@ -393,8 +408,6 @@
         return carry
 
     place_qkv(7)
-    qkv_copy(2).wait_send()
-    qkv_copy(3).wait_send()
     lax.fori_loop(0, 7, send_gn, 0)
     lax.fori_loop(0, 3, send_cot, 0)
     for i in range(8):
@@ -419,6 +432,17 @@
             silu = scores * sig
             probs[rows, cols] = silu.astype(BF16)
             slope[rows, cols] = sig + silu * (1.0 - sig)
+
+    def place_v(j, carry):
+        low, high = halves(seq_head(j))
+        value[low, :] = recv_qkv[j, :HALF, :HEAD]
+        value[high, :] = recv_qkv[j, HALF:, :HEAD]
+        return carry
+
+    wait_bytes(recv_qkv.at[pl.ds(0, 7), :, pl.ds(0, HEAD)], v_rs)
+    lax.fori_loop(0, SEQ, place_v, 0)
+    for i in range(4):
+        rows = pl.ds(i * STEP, STEP)
         seen = (i + 1) * STEP
         attn[rows, :] = dot(probs[rows, :seen], value[:seen, :])
 
@@ -650,6 +674,13 @@
 
     lax.fori_loop(0, 15, send_hist, 0)
 
+    for c in range(4):
+        cols = pl.ds(c * STEP, STEP)
+        layer_out_rows[:, cols] = dot(mixed[...], w_out[:, cols]).astype(BF16)
+        ig_acc[:, cols] = dot_t(gp_gate[...], w_gate[cols, :])
+    layer_out_copy = pltpu.make_async_copy(layer_out_rows, layer_out_ref.at[0], store_sem.at[0])
+    layer_out_copy.start()
+
     wait_bytes(mixed_all.at[:7], mixed_rs)
     cot_core.wait_recv()
     for g in range(8):
@@ -680,13 +711,6 @@
         return carry
 
     lax.fori_loop(0, 15, send_piece, 0)
-
-    for c in range(4):
-        cols = pl.ds(c * STEP, STEP)
-        layer_out_rows[:, cols] = dot(mixed[...], w_out[:, cols]).astype(BF16)
-        ig_acc[:, cols] = dot_t(gp_gate[...], w_gate[cols, :])
-    layer_out_copy = pltpu.make_async_copy(layer_out_rows, layer_out_ref.at[0], store_sem.at[0])
-    layer_out_copy.start()
 
     def add_head(j):
         grad_pre = (recv_dqkv[j].astype(F32) * slope_qkv[j]).astype(BF16)
@@ -771,8 +795,8 @@
     wait_bytes(hist_recv.at[:15], hist_ss)
     wait_bytes(cot_all.at[:3], cot_ss)
     cot_core.wait_send()
-    for k in range(4, 7):
-        qkv_copy(k).wait_send()
+    wait_bytes(recv_qkv.at[pl.ds(0, 7), :, pl.ds(HEAD, 2 * HEAD)], qkv_ss)
+    wait_bytes(recv_qkv.at[pl.ds(0, 7), :, pl.ds(0, HEAD)], v_ss)
     wait_bytes(recv_dqkv.at[pl.ds(0, 7), :, pl.ds(HEAD, 2 * HEAD)], dqkv_ss)
     wait_bytes(recv_dqkv.at[pl.ds(0, 7), :, pl.ds(0, HEAD)], dv_ss)
     layer_out_copy.wait()
@@ -848,16 +872,18 @@
         dma((2,)),
         dma((3,)),
         dma((12,)),
+        dma,
         dma((7,)),
+        dma,
+        dma,
+        dma,
+        dma,
+        dma,
+        dma,
+        dma,
         dma((7,)),
         dma,
         dma,
-        dma,
-        dma,
-        dma,
-        dma,
-        dma,
-        dma((7,)),
         dma,
         dma,
         dma,

time: 52.3 us -> 52.3 us (level)
  no operation moved by 1% of the time
where the time goes in v6:
time: 52.3 us; the launch traced here: 52.1 us
  Pallas kernels  51.5 us (98%)
  between operations  0.64 us (1%)
    pallas_call x1, Pallas kernels, body(): pl.pallas_call(kernel, out_shape=shapes, in_specs=[hbm] * 7, out_specs=(h...  49.7 us
    pallas_call x1, Pallas kernels, body(): pl.pallas_call(finish, out_shape=shapes, in_specs=[local] * 4, out_specs=...  1.85 us

profile of v6, /device:TPU:1, one launch (start us, length us, event | category | flops | bytes accessed | tf_op | source)
XLA Modules:
  0.0 52.1 jit_solution(4003389550249261738)
XLA Ops:
  0.6 49.7 %shard_map.102 = (bf16[1,128,1024]{2,1,0:T(8,128)(2,1)}, bf16[1,128,1024]{2,1,0:T(8,128)(2,1)}, f32[8,1024]{1,0:T(8,128)}, f32[8,18]{1,0:T(8,128)}) custom-call(bf16[1,128,1024]{2,1,0:T(8,128)(2,1)} %events_ref.1, bf16[1024,4096]{1,0:T(8,128)(2,1)} %in_weight_ref.1, bf16[1024,1024]{1,0:T(8,128)(2,1)} %out_weight_ref.1, f32[8,18]{1,0:T(8,128)} %bitcast.3, ...), custom_call_target="tpu_custom_call" | custom-call | tf_op jit(solution)/shard_map/pallas_call | solution.py:912
  50.3 1.8 %shard_map.103 = (bf16[1,128,1024]{2,1,0:T(8,128)(2,1)}, bf16[1,128,1024]{2,1,0:T(8,128)(2,1)}, f32[8,1024]{1,0:T(8,128)}, f32[8,18]{1,0:T(8,128)}) custom-call(bf16[1,128,1024]{2,1,0:T(8,128)(2,1)} %get-tuple-element.12.refs_0_, bf16[1,128,1024]{2,1,0:T(8,128)(2,1)} %get-tuple-element.13.refs_1_, f32[8,1024]{1,0:T(8,128)} %get-tuple-element.14.refs_2_, ...), custom_call_target="tpu_custom_call" | custom-call | tf_op jit(solution)/shard_map/pallas_call | solution.py:922
